TPU v7x, 32 devices: a whole 2x2x4 slice. The times are simulated.
32 devices in a mesh: rows: 16 (over z, x, core), seq: 2 (over y).
Axes of the slice: x: 2, y: 2, z: 4, core: 2. Of those that a mesh axis runs over, the one named last changes fastest.
Arguments:
- block_input: bfloat16 [64, 2048, 768], P('rows', 'seq'), may hold values from -6 to 6
- segment_ids: int32 [64, 2048], P('rows', 'seq'), may hold values from 0 to 3, as said below
- norm1_gain: float32 [768], replicated, may hold values from 0.1 to 1.9
- norm1_shift: float32 [768], replicated, may hold values from -3 to 3
- qkv_weight: bfloat16 [768, 2304], replicated, may hold values from -0.21875 to 0.21875
- qv_bias: float32 [1536], replicated, may hold values from -3 to 3
- proj_weight: bfloat16 [768, 768], replicated, may hold values from -6 to 6
- proj_bias: float32 [768], replicated, may hold values from -3 to 3
- norm2_gain: float32 [768], replicated, may hold values from 0.1 to 1.9
- norm2_shift: float32 [768], replicated, may hold values from -3 to 3
- fc_weight: bfloat16 [768, 3072], replicated, may hold values from -0.21875 to 0.21875
- fc_bias: float32 [3072], replicated, may hold values from -3 to 3
- out_weight: bfloat16 [3072, 768], replicated, may hold values from -0.3125 to 0.3125
- out_bias: float32 [768], replicated, may hold values from -3 to 3
- out_cotangent: bfloat16 [64, 2048, 768], P('rows', 'seq'), may hold values from -6 to 6
Outputs:
- layer_output: bfloat16 [64, 2048, 768], P('rows', 'seq')
- input_grad: float32 [64, 2048, 768], P('rows', 'seq')
- grad_norm1_gain: float32 [768], replicated
- grad_norm1_shift: float32 [768], replicated
- grad_qkv_weight: float32 [768, 2304], replicated
- grad_qv_bias: float32 [1536], replicated
- grad_proj_weight: float32 [768, 768], replicated
- grad_proj_bias: float32 [768], replicated
- grad_norm2_gain: float32 [768], replicated
- grad_norm2_shift: float32 [768], replicated
- grad_fc_weight: float32 [768, 3072], replicated
- grad_fc_bias: float32 [3072], replicated
- grad_out_weight: float32 [3072, 768], replicated
- grad_out_bias: float32 [768], replicated
Inputs may be any that keep to these rules, and one draw needn't show every extreme that they name: `segment_ids`: along each row the ids never fall; every row holds documents 0, 1 and 2 in that order, then padding marked 3 that ends the row.
All inputs are finite; a program needn't handle non-finite values.
Results may differ from a plain program's by a relative error of at most 0.02.
Values may be sent and summed in bfloat16 or wider, within the bound.
A program may use at most 576 MiB of HBM per device.

v0:
```python
from functools import partial, reduce

import jax
import jax.numpy as jnp
from jax import lax
from jax.experimental import pallas as pl
from jax.experimental.pallas import tpu as pltpu
from jax.sharding import PartitionSpec as P

HEADS = 12
HEAD_DIM = 64


BRANCH = 12 ** (-0.5)
EPSILON = 1e-05
PADDING = 3.0
NEGATIVE = -1e30
block_keys = 256


def layer_norm(values, scale_gain, shift_bias):
    center = values - jnp.mean(values, axis=-1, keepdims=True)
    variance = jnp.mean(center * center, axis=-1, keepdims=True)
    return center * lax.rsqrt(variance + EPSILON) * scale_gain + shift_bias


def allowed_pairs(query_segments, key_segments, query_slots, key_slots):
    same_doc = query_segments[:, :, None] == key_segments[:, None, :]
    causal = key_slots[None, None, :] <= query_slots[None, :, None]
    itself = key_slots[None, None, :] == query_slots[None, :, None]
    unpadded = key_segments[:, None, :] != PADDING
    return (same_doc & causal & (unpadded | itself))[:, None]


def split_heads(block_rows):
    return block_rows.reshape(block_rows.shape[0], block_rows.shape[1], HEADS, HEAD_DIM)


def fold_blocks(block_step, running, piece_tuple):
    piece_len = piece_tuple[0].shape[1]

    def one_block(block_index, held_state):
        offset = block_index * block_keys
        sub_tuple = tuple(
            (lax.dynamic_slice_in_dim(member, offset, block_keys, 1) for member in piece_tuple)
        )
        return block_step(held_state, sub_tuple, offset)

    return lax.fori_loop(0, piece_len // block_keys, one_block, running)


def keep_same(running):
    return running


def local(
    block_input,
    segment_ids,
    norm1_gain,
    norm1_shift,
    qkv_weight,
    qv_bias,
    proj_weight,
    proj_bias,
    norm2_gain,
    norm2_shift,
    fc_weight,
    fc_bias,
    out_weight,
    out_bias,
    out_cotangent,
):
    row_count, local_len, model_width = block_input.shape
    tokens = row_count * local_len
    full_len = local_len * lax.axis_size("seq")
    my_first = lax.axis_index("seq") * local_len
    query_slots = my_first + jnp.arange(local_len)
    my_segments = segment_ids.astype(jnp.bfloat16)
    my_seg_float = segment_ids.astype(jnp.float32)
    score_scale = HEAD_DIM ** (-0.5)
    inputs = block_input.astype(jnp.float32).reshape(tokens, model_width)
    normed_one = layer_norm(inputs, norm1_gain, norm1_shift).astype(jnp.bfloat16)
    mixed_qkv = jnp.dot(normed_one, qkv_weight, preferred_element_type=jnp.float32)
    query_flat = (
        (mixed_qkv[:, :model_width] + qv_bias[:model_width])
        .astype(jnp.bfloat16)
        .reshape(row_count, local_len, model_width)
    )
    key_rows = (
        mixed_qkv[:, model_width : 2 * model_width]
        .astype(jnp.bfloat16)
        .reshape(row_count, local_len, model_width)
    )
    value_rows = (
        (mixed_qkv[:, 2 * model_width :] + qv_bias[model_width:])
        .astype(jnp.bfloat16)
        .reshape(row_count, local_len, model_width)
    )
    queries = split_heads(query_flat)

    def attend_block(running, sub_tuple, first_slot):
        key_piece, value_piece, seg_piece = sub_tuple
        piece_len = key_piece.shape[1]
        key_slots = first_slot + jnp.arange(piece_len)
        seg_float = seg_piece.astype(jnp.float32)
        skipped = (first_slot > my_first + local_len - 1) | (
            jnp.max(seg_float) < jnp.min(my_seg_float)
        )

        def attend_update(state):
            running_max, running_sum, running_out = state
            scores = (
                jnp.einsum(
                    "rqhd,rkhd->rhqk",
                    queries,
                    split_heads(key_piece),
                    preferred_element_type=jnp.float32,
                )
                * score_scale
            )
            allowed = allowed_pairs(my_seg_float, seg_float, query_slots, key_slots)
            masked = jnp.where(allowed, scores, NEGATIVE)
            new_max = jnp.maximum(running_max, jnp.max(masked, axis=-1))
            prob_block = jnp.where(allowed, jnp.exp(scores - new_max[..., None]), 0.0)
            factor = jnp.exp(running_max - new_max)
            new_sum = running_sum * factor + jnp.sum(prob_block, axis=-1)
            added_part = jnp.einsum(
                "rhqk,rkhd->rqhd",
                prob_block.astype(jnp.bfloat16),
                split_heads(value_piece),
                preferred_element_type=jnp.float32,
            )
            new_out = running_out * jnp.transpose(factor, (0, 2, 1))[..., None] + added_part
            return (new_max, new_sum, new_out)

        return lax.cond(skipped, keep_same, attend_update, running)

    start_state = (
        jnp.full((row_count, HEADS, local_len), NEGATIVE, jnp.float32),
        jnp.zeros((row_count, HEADS, local_len), jnp.float32),
        jnp.zeros((row_count, local_len, HEADS, HEAD_DIM), jnp.float32),
    )
    running_max, running_sum, running_out = fold_blocks(
        attend_block,
        start_state,
        (
            lax.all_gather(key_rows, "seq", axis=1, tiled=True),
            lax.all_gather(value_rows, "seq", axis=1, tiled=True),
            lax.all_gather(my_segments, "seq", axis=1, tiled=True),
        ),
    )
    log_total = running_max + jnp.log(running_sum)
    attended_heads = running_out / jnp.transpose(running_sum, (0, 2, 1))[..., None]
    attended_low = attended_heads.reshape(tokens, model_width).astype(jnp.bfloat16)
    branch_one = jnp.dot(attended_low, proj_weight, preferred_element_type=jnp.float32) + proj_bias
    middle = inputs + BRANCH * branch_one
    normed_two = layer_norm(middle, norm2_gain, norm2_shift).astype(jnp.bfloat16)
    hidden_pre = jnp.dot(normed_two, fc_weight, preferred_element_type=jnp.float32) + fc_bias
    hidden_act = jax.nn.gelu(hidden_pre, approximate=True).astype(jnp.bfloat16)
    branch_two = jnp.dot(hidden_act, out_weight, preferred_element_type=jnp.float32) + out_bias
    layer_output = (
        (middle + BRANCH * branch_two)
        .astype(jnp.bfloat16)
        .reshape(row_count, local_len, model_width)
    )
    flat_cot = out_cotangent.reshape(tokens, model_width).astype(jnp.float32)
    grad_two = (BRANCH * flat_cot).astype(jnp.bfloat16)
    grad_out_weight = jnp.einsum(
        "tf,td->fd", hidden_act, grad_two, preferred_element_type=jnp.float32
    )
    grad_out_bias = jnp.sum(grad_two.astype(jnp.float32), axis=0)
    grad_act = jnp.einsum("td,fd->tf", grad_two, out_weight, preferred_element_type=jnp.float32)
    gelu_value, gelu_pull = jax.vjp(partial(jax.nn.gelu, approximate=True), hidden_pre)
    grad_pre = gelu_pull(grad_act)[0].astype(jnp.bfloat16)
    grad_fc_weight = jnp.einsum(
        "td,tf->df", normed_two, grad_pre, preferred_element_type=jnp.float32
    )
    grad_fc_bias = jnp.sum(grad_pre.astype(jnp.float32), axis=0)
    grad_normed_two = jnp.einsum(
        "tf,df->td", grad_pre, fc_weight, preferred_element_type=jnp.float32
    )
    norm_value, norm_pull = jax.vjp(layer_norm, middle, norm2_gain, norm2_shift)
    grad_inner, grad_norm2_gain, grad_norm2_shift = norm_pull(grad_normed_two)
    grad_middle = flat_cot + grad_inner
    grad_one = (BRANCH * grad_middle).astype(jnp.bfloat16)
    grad_proj_weight = jnp.einsum(
        "td,te->de", attended_low, grad_one, preferred_element_type=jnp.float32
    )
    grad_proj_bias = jnp.sum(grad_one.astype(jnp.float32), axis=0)
    grad_attended_flat = (
        jnp.einsum("te,de->td", grad_one, proj_weight, preferred_element_type=jnp.float32)
        .astype(jnp.bfloat16)
        .reshape(row_count, local_len, model_width)
    )
    grad_attended = split_heads(grad_attended_flat)
    grad_delta = jnp.einsum("rqhd,rqhd->rhq", grad_attended.astype(jnp.float32), attended_heads)

    def back_block(running, sub_tuple, first_slot):
        key_piece, value_piece, seg_piece = sub_tuple
        piece_len = key_piece.shape[1]
        key_slots = first_slot + jnp.arange(piece_len)
        seg_float = seg_piece.astype(jnp.float32)
        skipped = (first_slot > my_first + local_len - 1) | (
            jnp.max(seg_float) < jnp.min(my_seg_float)
        )

        def back_update(state):
            grad_query, grad_full = state
            key_heads = split_heads(key_piece)
            value_heads = split_heads(value_piece)
            scores = (
                jnp.einsum(
                    "rqhd,rkhd->rhqk", queries, key_heads, preferred_element_type=jnp.float32
                )
                * score_scale
            )
            allowed = allowed_pairs(my_seg_float, seg_float, query_slots, key_slots)
            prob_block = jnp.where(allowed, jnp.exp(scores - log_total[..., None]), 0.0)
            grad_probs = jnp.einsum(
                "rqhd,rkhd->rhqk", grad_attended, value_heads, preferred_element_type=jnp.float32
            )
            grad_scores = (score_scale * prob_block * (grad_probs - grad_delta[..., None])).astype(
                jnp.bfloat16
            )
            new_query = grad_query + jnp.einsum(
                "rhqk,rkhd->rqhd", grad_scores, key_heads, preferred_element_type=jnp.float32
            )
            grad_keys = jnp.einsum(
                "rhqk,rqhd->rkhd", grad_scores, queries, preferred_element_type=jnp.float32
            ).reshape(row_count, piece_len, model_width)
            grad_values = jnp.einsum(
                "rhqk,rqhd->rkhd",
                prob_block.astype(jnp.bfloat16),
                grad_attended,
                preferred_element_type=jnp.float32,
            ).reshape(row_count, piece_len, model_width)
            held_part = lax.dynamic_slice_in_dim(grad_full, first_slot, piece_len, 2)
            new_full = lax.dynamic_update_slice_in_dim(
                grad_full, held_part + jnp.stack((grad_keys, grad_values)), first_slot, 2
            )
            return (new_query, new_full)

        return lax.cond(skipped, keep_same, back_update, running)

    back_start = (
        jnp.zeros((row_count, local_len, HEADS, HEAD_DIM), jnp.float32),
        jnp.zeros((2, row_count, full_len, model_width), jnp.float32),
    )
    grad_query, grad_full = fold_blocks(
        back_block,
        back_start,
        (
            lax.all_gather(key_rows, "seq", axis=1, tiled=True),
            lax.all_gather(value_rows, "seq", axis=1, tiled=True),
            lax.all_gather(my_segments, "seq", axis=1, tiled=True),
        ),
    )
    grad_pairs = lax.psum_scatter(
        grad_full.astype(jnp.bfloat16), "seq", scatter_dimension=2, tiled=True
    ).astype(jnp.float32)
    grad_query_low = grad_query.reshape(row_count, local_len, model_width).astype(jnp.bfloat16)
    grad_key_low = grad_pairs[0].astype(jnp.bfloat16)
    grad_value_low = grad_pairs[1].astype(jnp.bfloat16)
    grad_qkv_low = jnp.concatenate((grad_query_low, grad_key_low, grad_value_low), axis=-1).reshape(
        tokens, 3 * model_width
    )
    grad_qkv_weight = jnp.einsum(
        "td,te->de", normed_one, grad_qkv_low, preferred_element_type=jnp.float32
    )
    grad_qv_bias = jnp.concatenate(
        (
            jnp.sum(grad_query_low.astype(jnp.float32), axis=(0, 1)),
            jnp.sum(grad_value_low.astype(jnp.float32), axis=(0, 1)),
        )
    )
    grad_normed_one = jnp.einsum(
        "te,de->td", grad_qkv_low, qkv_weight, preferred_element_type=jnp.float32
    )
    first_value, first_pull = jax.vjp(layer_norm, inputs, norm1_gain, norm1_shift)
    grad_first, grad_norm1_gain, grad_norm1_shift = first_pull(grad_normed_one)
    input_grad = (grad_middle + grad_first).reshape(row_count, local_len, model_width)
    local_grads = (
        grad_norm1_gain,
        grad_norm1_shift,
        grad_qkv_weight,
        grad_qv_bias,
        grad_proj_weight,
        grad_proj_bias,
        grad_norm2_gain,
        grad_norm2_shift,
        grad_fc_weight,
        grad_fc_bias,
        grad_out_weight,
        grad_out_bias,
    )
    shares = (
        lax.psum_scatter(
            local_grads[0].astype(jnp.bfloat16), "rows", scatter_dimension=0, tiled=True
        ).astype(jnp.float32),
        lax.psum_scatter(
            local_grads[1].astype(jnp.bfloat16), "rows", scatter_dimension=0, tiled=True
        ).astype(jnp.float32),
        lax.psum_scatter(
            local_grads[2].astype(jnp.bfloat16), "rows", scatter_dimension=0, tiled=True
        ).astype(jnp.float32),
        lax.psum_scatter(
            local_grads[3].astype(jnp.bfloat16), "rows", scatter_dimension=0, tiled=True
        ).astype(jnp.float32),
        lax.psum_scatter(
            local_grads[4].astype(jnp.bfloat16), "rows", scatter_dimension=0, tiled=True
        ).astype(jnp.float32),
        lax.psum_scatter(
            local_grads[5].astype(jnp.bfloat16), "rows", scatter_dimension=0, tiled=True
        ).astype(jnp.float32),
        lax.psum_scatter(
            local_grads[6].astype(jnp.bfloat16), "rows", scatter_dimension=0, tiled=True
        ).astype(jnp.float32),
        lax.psum_scatter(
            local_grads[7].astype(jnp.bfloat16), "rows", scatter_dimension=0, tiled=True
        ).astype(jnp.float32),
        lax.psum_scatter(
            local_grads[8].astype(jnp.bfloat16), "rows", scatter_dimension=0, tiled=True
        ).astype(jnp.float32),
        lax.psum_scatter(
            local_grads[9].astype(jnp.bfloat16), "rows", scatter_dimension=0, tiled=True
        ).astype(jnp.float32),
        lax.psum_scatter(
            local_grads[10].astype(jnp.bfloat16), "rows", scatter_dimension=0, tiled=True
        ).astype(jnp.float32),
        lax.psum_scatter(
            local_grads[11].astype(jnp.bfloat16), "rows", scatter_dimension=0, tiled=True
        ).astype(jnp.float32),
    )
    shares = (
        lax.psum(shares[0].astype(jnp.bfloat16), "seq").astype(jnp.float32),
        lax.psum(shares[1].astype(jnp.bfloat16), "seq").astype(jnp.float32),
        lax.psum(shares[2].astype(jnp.bfloat16), "seq").astype(jnp.float32),
        lax.psum(shares[3].astype(jnp.bfloat16), "seq").astype(jnp.float32),
        lax.psum(shares[4].astype(jnp.bfloat16), "seq").astype(jnp.float32),
        lax.psum(shares[5].astype(jnp.bfloat16), "seq").astype(jnp.float32),
        lax.psum(shares[6].astype(jnp.bfloat16), "seq").astype(jnp.float32),
        lax.psum(shares[7].astype(jnp.bfloat16), "seq").astype(jnp.float32),
        lax.psum(shares[8].astype(jnp.bfloat16), "seq").astype(jnp.float32),
        lax.psum(shares[9].astype(jnp.bfloat16), "seq").astype(jnp.float32),
        lax.psum(shares[10].astype(jnp.bfloat16), "seq").astype(jnp.float32),
        lax.psum(shares[11].astype(jnp.bfloat16), "seq").astype(jnp.float32),
    )
    totals = (
        lax.all_gather(shares[0].astype(jnp.bfloat16), "rows", axis=0, tiled=True).astype(
            jnp.float32
        ),
        lax.all_gather(shares[1].astype(jnp.bfloat16), "rows", axis=0, tiled=True).astype(
            jnp.float32
        ),
        lax.all_gather(shares[2].astype(jnp.bfloat16), "rows", axis=0, tiled=True).astype(
            jnp.float32
        ),
        lax.all_gather(shares[3].astype(jnp.bfloat16), "rows", axis=0, tiled=True).astype(
            jnp.float32
        ),
        lax.all_gather(shares[4].astype(jnp.bfloat16), "rows", axis=0, tiled=True).astype(
            jnp.float32
        ),
        lax.all_gather(shares[5].astype(jnp.bfloat16), "rows", axis=0, tiled=True).astype(
            jnp.float32
        ),
        lax.all_gather(shares[6].astype(jnp.bfloat16), "rows", axis=0, tiled=True).astype(
            jnp.float32
        ),
        lax.all_gather(shares[7].astype(jnp.bfloat16), "rows", axis=0, tiled=True).astype(
            jnp.float32
        ),
        lax.all_gather(shares[8].astype(jnp.bfloat16), "rows", axis=0, tiled=True).astype(
            jnp.float32
        ),
        lax.all_gather(shares[9].astype(jnp.bfloat16), "rows", axis=0, tiled=True).astype(
            jnp.float32
        ),
        lax.all_gather(shares[10].astype(jnp.bfloat16), "rows", axis=0, tiled=True).astype(
            jnp.float32
        ),
        lax.all_gather(shares[11].astype(jnp.bfloat16), "rows", axis=0, tiled=True).astype(
            jnp.float32
        ),
    )
    return (layer_output, input_grad) + tuple(totals)


MIB = 1 << 20
LOG2E = 1.4426950408889634
GELU_C = 0.7978845608028654
GELU_A = 0.044715
BLOCK = 256
f32 = jnp.float32
bf16 = jnp.bfloat16


def dot_nn(a, b):
    return lax.dot_general(a, b, (((1,), (0,)), ((), ())), preferred_element_type=f32)


def dot_tn(a, b):
    return lax.dot_general(a, b, (((0,), (0,)), ((), ())), preferred_element_type=f32)


def dot_nt(a, b):
    return lax.dot_general(a, b, (((1,), (1,)), ((), ())), preferred_element_type=f32)


def norm_parts(values):
    center = values - jnp.mean(values, axis=-1, keepdims=True)
    variance = jnp.mean(center * center, axis=-1, keepdims=True)
    inverse = lax.rsqrt(variance + EPSILON)
    return center * inverse, inverse


def row_sums(values):
    rows, cols = values.shape
    return jnp.sum(values.reshape(rows // 8, 8, cols), axis=0)


def whole(shape):
    return pl.BlockSpec(shape, lambda *_: (0,) * len(shape), pipeline_mode=pl.Buffered(1))


def call(
    kernel, name, grid, in_specs, out_specs, out_shape, scratch, flops, moved, vmem, prefetch=1, aliases=None
):
    return pl.pallas_call(
        kernel,
        out_shape=out_shape,
        grid_spec=pltpu.PrefetchScalarGridSpec(
            num_scalar_prefetch=prefetch,
            grid=grid,
            in_specs=in_specs,
            out_specs=out_specs,
            scratch_shapes=scratch,
        ),
        compiler_params=pltpu.CompilerParams(vmem_limit_bytes=vmem * MIB),
        cost_estimate=pl.CostEstimate(flops=flops, bytes_accessed=moved, transcendentals=0),
        input_output_aliases=aliases or {},
        name=name,
    )


TILE = 512
LIMIT = 2.0**100


class Place:
    def __init__(self, rows, half_len):
        self.rows, self.per = rows, half_len // TILE
        self.phase = rows * self.per
        self.steps = 2 * self.phase

    def own(self, t, me):
        return me[0] * self.phase + jnp.minimum(t, self.phase - 1), 0

    def got(self, t, me):
        return jnp.maximum(t - self.phase, 0), 0

    def slot(self, t, me):
        late = t // self.phase
        half = jnp.where(late == 0, me[0], 1 - me[0])
        at = t - late * self.phase
        return (at // self.per) * 2 * self.per + half * self.per + at % self.per

    def turned(self, t, me):
        return 0, self.slot(t, me)

    def back(self, t, me):
        return (1 - me[0]) * self.phase + t, 0


def either(step, phase, own_ref, got_ref):
    return jnp.where(step < phase, own_ref[...], got_ref[...])


def qkv_kernel(me_ref, x_ref, gain_ref, shift_ref, w_ref, bias_ref, *refs):
    width = x_ref.shape[1]
    hat, _ = norm_parts(x_ref[...].astype(f32))
    normed = (hat * gain_ref[...] + shift_ref[...]).astype(bf16)
    for i, ref in enumerate(refs[-3:]):
        part = dot_nt(w_ref[i * width : (i + 1) * width, :], normed)
        if i != 1:
            part = part + bias_ref[i * width : (i + 1) * width, :]
        ref[...] = part.astype(bf16)


def project_qkv(me, x, params, place, first, count, got, earlier, after):
    width = x.shape[1]
    tokens = place.steps * TILE
    index = (lambda t, me: (t, 0)) if got else (lambda t, me: place.own(t + first, me))
    turned = pl.BlockSpec((width, TILE), lambda t, me: place.turned(t + first, me))
    anywhere = pl.BlockSpec(memory_space=pl.ANY)
    extra = list(earlier) + list(after)
    return call(
        qkv_kernel,
        "qkv_forward",
        (count,),
        [pl.BlockSpec((TILE, width), index)]
        + [whole(p.shape) for p in params]
        + [anywhere] * len(extra),
        [turned] * 3,
        [jax.ShapeDtypeStruct((width, tokens), bf16)] * 3,
        [],
        2 * count * TILE * width * 3 * width,
        count * TILE * width * 8 + width * width * 6,
        60,
        aliases={6 + i: i for i in range(len(earlier))},
    )(me, x, *params, *extra)


def attend_kernel(low_ref, start_ref, qt_ref, kt_ref, vt_ref, *refs, row, first, blocks):
    att_ref, lse_ref, acc, base, bias = refs[-5:]
    width, length = qt_ref.shape
    heads = width // HEAD_DIM
    pad = HEAD_DIM + 16
    scale = HEAD_DIM**-0.5 * LOG2E
    slots = lax.broadcasted_iota(jnp.int32, (BLOCK, BLOCK), 0)
    query_iota = lax.broadcasted_iota(jnp.int32, (BLOCK, BLOCK), 1)
    ones = jnp.ones((16, BLOCK), bf16)

    def at(i):
        return pl.ds(pl.multiple_of(i * BLOCK, BLOCK), BLOCK)

    def head_rows(h):
        return slice(h * HEAD_DIM, (h + 1) * HEAD_DIM)

    def acc_rows(h):
        return slice(h * pad, (h + 1) * pad)

    def total(h):
        return acc[h * pad + HEAD_DIM : h * pad + HEAD_DIM + 1, :]

    def score(h, qb, kb):
        return dot_tn(kt_ref[head_rows(h), at(kb)], qt_ref[head_rows(h), at(qb - first)])

    def weigh(h, kb, probs):
        return dot_nn(jnp.concatenate((vt_ref[head_rows(h), at(kb)], ones), axis=0), probs)

    def set_bias(qb, kb):
        allowed = (slots >= start_ref[0, :, at(qb - first)] - kb * BLOCK) & (
            slots + (kb - qb) * BLOCK <= query_iota
        )
        bias[...] = jnp.where(allowed, 0.0, NEGATIVE)

    def query_block(qb, carry):
        low = low_ref[row * blocks + qb]
        for h in range(heads):
            own = qt_ref[head_rows(h), at(qb - first)].astype(f32) * kt_ref[head_rows(h), at(qb)].astype(f32)
            base[h : h + 1, :] = jnp.sum(own, axis=0, keepdims=True) * scale
        acc[...] = jnp.zeros_like(acc)

        def fast(kb, carry):
            set_bias(qb, kb)

            def finish(h, probs):
                acc[acc_rows(h), :] += weigh(h, kb, probs)

            ahead = [score(h, qb, kb) for h in range(min(3, heads))]
            waiting = []
            for h in range(heads):
                scores = ahead.pop(0)
                if h + 3 < heads:
                    ahead.append(score(h + 3, qb, kb))
                probs = jnp.exp2(scores * scale + (bias[...] - base[h : h + 1, :]))
                waiting.append((h, probs.astype(bf16)))
                if len(waiting) > 1:
                    finish(*waiting.pop(0))
            finish(*waiting[0])
            return carry

        lax.fori_loop(low, qb + 1, fast, 0)
        largest = reduce(jnp.maximum, [total(h) for h in range(heads)])

        @pl.when(jnp.logical_not(jnp.max(largest) < LIMIT))
        def _():
            base[...] = jnp.full_like(base, NEGATIVE)
            acc[...] = jnp.zeros_like(acc)

            def safe(kb, carry):
                set_bias(qb, kb)
                for h in range(heads):
                    scores = score(h, qb, kb) * scale + bias[...]
                    old = base[h : h + 1, :]
                    top = jnp.maximum(old, jnp.max(scores, axis=0, keepdims=True))
                    base[h : h + 1, :] = top
                    probs = jnp.exp2(scores - top).astype(bf16)
                    acc[acc_rows(h), :] = acc[acc_rows(h), :] * jnp.exp2(old - top) + weigh(h, kb, probs)
                return carry

            lax.fori_loop(low, qb + 1, safe, 0)

        for h in range(heads):
            out = acc[h * pad : h * pad + HEAD_DIM, :]
            att_ref[head_rows(h), at(qb - first)] = (out / total(h)).astype(bf16)
            lse_ref[h // 2, h % 2 : h % 2 + 1, at(qb - first)] = base[h : h + 1, :] + jnp.log2(total(h))
        return carry

    lax.fori_loop(first, first + length // BLOCK, query_block, 0)


def attend(low, start, qt, kt, vt, row, length, part, parts, earlier):
    width, tokens = qt.shape
    heads = width // HEAD_DIM
    span = length // parts
    seen = span * (part + 1)
    column = row * parts + part
    queries = pl.BlockSpec((width, span), lambda i, low: (0, column))
    keys = pl.BlockSpec((width, seen), lambda i, low: (0, row * length // seen))
    lined = pl.BlockSpec((heads // 2, 2, span), lambda i, low: (0, 0, column))
    return call(
        partial(attend_kernel, row=row, first=part * span // BLOCK, blocks=length // BLOCK),
        "attention_forward",
        (1,),
        [pl.BlockSpec((1, 1, span), lambda i, low: (row, 0, part)), queries, keys, keys]
        + [pl.BlockSpec(memory_space=pl.ANY)] * len(earlier),
        [queries, lined],
        [
            jax.ShapeDtypeStruct((width, tokens), bf16),
            jax.ShapeDtypeStruct((heads // 2, 2, tokens), f32),
        ],
        [
            pltpu.VMEM((heads * (HEAD_DIM + 16), BLOCK), f32),
            pltpu.VMEM((16, BLOCK), f32),
            pltpu.VMEM((BLOCK, BLOCK), f32),
        ],
        2 * span * seen * width,
        length * width * 8,
        60,
        aliases={5 + i: i for i in range(len(earlier))},
    )(low, start, qt, kt, vt, *earlier)


def attend_back_kernel(
    high_ref, start_ref, qt_ref, kt_ref, vt_ref, dot_ref, lse_ref, delta_ref,
    dqt_ref, dkt_ref, dvt_ref, dq, dk, dv, bias,
):
    row = pl.program_id(0)
    width, length = qt_ref.shape
    heads = width // HEAD_DIM
    blocks = length // BLOCK
    scale = HEAD_DIM**-0.5 * LOG2E
    slots = lax.broadcasted_iota(jnp.int32, (BLOCK, BLOCK), 0)
    query_iota = lax.broadcasted_iota(jnp.int32, (BLOCK, BLOCK), 1)
    dq[...] = jnp.zeros_like(dq)

    def at(i):
        return pl.ds(pl.multiple_of(i * BLOCK, BLOCK), BLOCK)

    def key_block(kb, carry):
        k_at = at(kb)

        def visit(qb, first):
            q_at = at(qb)
            allowed = slots >= start_ref[0, :, q_at] - kb * BLOCK
            if first:
                allowed = allowed & (slots <= query_iota)
            bias[...] = jnp.where(allowed, 0.0, NEGATIVE)

            def begin(h):
                rows = slice(h * HEAD_DIM, (h + 1) * HEAD_DIM)
                return (
                    dot_tn(kt_ref[rows, k_at], qt_ref[rows, q_at]),
                    dot_tn(vt_ref[rows, k_at], dot_ref[rows, q_at]),
                )

            def finish(h, probs, grad_scores):
                rows = slice(h * HEAD_DIM, (h + 1) * HEAD_DIM)
                dv_new = dot_nt(dot_ref[rows, q_at], probs)
                dk_new = dot_nt(qt_ref[rows, q_at], grad_scores)
                dv[rows, :] = dv_new if first else dv[rows, :] + dv_new
                dk[rows, :] = dk_new if first else dk[rows, :] + dk_new
                dq[rows, q_at] += dot_nn(kt_ref[rows, k_at], grad_scores)

            ahead = [begin(0)]
            waiting = []
            for h in range(heads):
                scores, grad_probs = ahead.pop(0)
                if h + 1 < heads:
                    ahead.append(begin(h + 1))
                line = (h // 2, slice(h % 2, h % 2 + 1), q_at)
                probs = jnp.exp2(scores * scale + (bias[...] - lse_ref[line]))
                grad_scores = (probs * (grad_probs - delta_ref[line])).astype(bf16)
                waiting.append((h, probs.astype(bf16), grad_scores))
                if len(waiting) > 1:
                    finish(*waiting.pop(0))
            finish(*waiting[0])

        visit(kb, True)

        def later(qb, carry):
            visit(qb, False)
            return carry

        lax.fori_loop(kb + 1, high_ref[row * blocks + kb] + 1, later, 0)
        dkt_ref[:, k_at] = (dk[...] * HEAD_DIM**-0.5).astype(bf16)
        dvt_ref[:, k_at] = dv[...].astype(bf16)
        return carry

    lax.fori_loop(0, blocks, key_block, 0)
    dqt_ref[...] = (dq[...] * HEAD_DIM**-0.5).astype(bf16)


def attend_back(high, start, qt, kt, vt, dot, lse, delta, rows):
    width, tokens = qt.shape
    length = tokens // rows
    heads = width // HEAD_DIM
    turned = pl.BlockSpec((width, length), lambda r, high: (0, r))
    lined = pl.BlockSpec((heads // 2, 2, length), lambda r, high: (0, 0, r))
    return call(
        attend_back_kernel,
        "attention_backward",
        (rows,),
        [pl.BlockSpec((1, 1, length), lambda r, high: (r, 0, 0)), turned, turned, turned, turned, lined, lined],
        [turned] * 3,
        [jax.ShapeDtypeStruct((width, tokens), bf16)] * 3,
        [
            pltpu.VMEM((width, length), f32),
            pltpu.VMEM((width, BLOCK), f32),
            pltpu.VMEM((width, BLOCK), f32),
            pltpu.VMEM((BLOCK, BLOCK), f32),
        ],
        5 * tokens * length * width,
        tokens * width * 14,
        62,
    )(high, start, qt, kt, vt, dot, lse, delta)


def mlp_kernel(
    me_ref, x_ref, xg_ref, cot_ref, cotg_ref, att_ref, proj_ref, projb_ref, gain_ref, shift_ref, fc_ref, fcb_ref,
    out_ref, outb_ref,
    kept_ref, sent_ref, gm_ref, do_ref, delta_ref, dfc_ref, dout_ref, dproj_ref, small_ref, dfcb_ref,
    dfc, doutt, dproj, sums, dfcb, stage, sem,
):
    step = pl.program_id(0)
    steps = pl.num_programs(0)
    phase = steps // 2
    tile, width = x_ref.shape
    hidden = fc_ref.shape[1]
    chunk = 768

    @pl.when(step == 0)
    def _():
        dfc[...] = jnp.zeros_like(dfc)
        doutt[...] = jnp.zeros_like(doutt)
        dproj[...] = jnp.zeros_like(dproj)
        sums[...] = jnp.zeros_like(sums)
        dfcb[...] = jnp.zeros_like(dfcb)

    att_t = att_ref[...]
    x = either(step, phase, x_ref, xg_ref).astype(f32)
    middle = x + BRANCH * (dot_tn(att_t, proj_ref[...]) + projb_ref[...])
    hat, inverse = norm_parts(middle)
    normed = (hat * gain_ref[...] + shift_ref[...]).astype(bf16)
    normed_t = jnp.transpose(normed)
    cot = either(step, phase, cot_ref, cotg_ref).astype(f32)
    grad_two = (BRANCH * cot).astype(bf16)
    grad_two_t = jnp.transpose(grad_two)
    branch = jnp.zeros((tile, width), f32)
    grad_normed = jnp.zeros((tile, width), f32)
    for at in range(0, hidden, chunk):
        cols = slice(at, at + chunk)
        pre = dot_nn(normed, fc_ref[:, cols]) + fcb_ref[:, cols]
        grad_act = dot_nt(grad_two, out_ref[cols, :])
        square = pre * pre
        half = 0.5 + 0.5 * jnp.tanh(pre * (GELU_C + GELU_C * GELU_A * square))
        act = pre * half
        slope = half + act * (1.0 - half) * (2.0 * GELU_C + 6.0 * GELU_C * GELU_A * square)
        act = act.astype(bf16)
        grad_pre = (grad_act * slope).astype(bf16)
        branch += dot_nn(act, out_ref[cols, :])
        grad_normed += dot_nt(grad_pre, fc_ref[:, cols])
        dfc[:, cols] += dot_nn(normed_t, grad_pre)
        doutt[:, cols] += dot_nn(grad_two_t, act)
        dfcb[:, cols] += row_sums(grad_pre.astype(f32))
    y = (middle + BRANCH * (branch + outb_ref[...])).astype(bf16)

    @pl.when(step < phase)
    def _():
        kept_ref[...] = y

    @pl.when(step >= phase)
    def _():
        sent_ref[...] = y

    scaled = grad_normed * gain_ref[...]
    mean_one = jnp.mean(scaled, axis=-1, keepdims=True)
    mean_two = jnp.mean(scaled * hat, axis=-1, keepdims=True)
    grad_middle = cot + inverse * (scaled - mean_one - hat * mean_two)
    gm_ref[...] = grad_middle.astype(bf16)
    grad_one = (BRANCH * grad_middle).astype(bf16)
    dproj[...] += dot_nn(att_t, grad_one)
    grad_att = dot_nt(proj_ref[...], grad_one).astype(bf16)
    do_ref[...] = grad_att
    product = grad_att.astype(f32) * att_t.astype(f32)
    for h in range(width // HEAD_DIM):
        part = product[h * HEAD_DIM : (h + 1) * HEAD_DIM, :]
        delta_ref[h // 2, h % 2 : h % 2 + 1, :] = jnp.sum(part, axis=0, keepdims=True)
    sums[0:8, :] += row_sums(grad_normed * hat)
    sums[8:16, :] += row_sums(grad_normed)
    sums[16:24, :] += row_sums(grad_two.astype(f32))
    sums[24:32, :] += row_sums(grad_one.astype(f32))

    @pl.when(step == steps - 1)
    def _():
        for at in range(0, hidden, chunk):
            cols = slice(at, at + chunk)
            stage[...] = dfc[:, cols].astype(bf16)
            copy = pltpu.make_async_copy(stage, dfc_ref.at[:, cols], sem)
            copy.start()
            copy.wait()
            stage[...] = jnp.transpose(doutt[:, cols].astype(bf16))
            copy = pltpu.make_async_copy(stage, dout_ref.at[cols, :], sem)
            copy.start()
            copy.wait()
        dproj_ref[...] = dproj[...].astype(bf16)
        small_ref[...] = sums[...]
        dfcb_ref[...] = dfcb[...]


def feed_forward(
    me, x, x_got, cot, cot_got, att, place, proj_weight, proj_bias, gain, shift, fc_weight, fc_bias, out_weight, out_bias
):
    width, tokens = att.shape
    hidden = fc_weight.shape[1]
    heads = width // HEAD_DIM
    own = pl.BlockSpec((TILE, width), place.own)
    got = pl.BlockSpec((TILE, width), place.got)
    turned = pl.BlockSpec((width, TILE), place.turned)
    plain = pl.BlockSpec((TILE, width), lambda t, me: (t, 0))
    anywhere = pl.BlockSpec(memory_space=pl.ANY)
    return call(
        mlp_kernel,
        "feed_forward",
        (place.steps,),
        [own, got, own, got, turned, whole((width, width)), whole((1, width)), whole((1, width)), whole((1, width)),
         whole(fc_weight.shape), whole((1, hidden)), whole(out_weight.shape), whole((1, width))],
        [own, got, plain, turned,
         pl.BlockSpec((heads // 2, 2, TILE), lambda t, me: (0, 0, place.slot(t, me))),
         anywhere, anywhere, whole((width, width)), whole((32, width)), whole((8, hidden))],
        [
            jax.ShapeDtypeStruct((tokens, width), bf16),
            jax.ShapeDtypeStruct((tokens // 2, width), bf16),
            jax.ShapeDtypeStruct((tokens, width), bf16),
            jax.ShapeDtypeStruct((width, tokens), bf16),
            jax.ShapeDtypeStruct((heads // 2, 2, tokens), f32),
            jax.ShapeDtypeStruct((width, hidden), bf16),
            jax.ShapeDtypeStruct((hidden, width), bf16),
            jax.ShapeDtypeStruct((width, width), bf16),
            jax.ShapeDtypeStruct((32, width), f32),
            jax.ShapeDtypeStruct((8, hidden), f32),
        ],
        [
            pltpu.VMEM((width, hidden), f32),
            pltpu.VMEM((width, hidden), f32),
            pltpu.VMEM((width, width), f32),
            pltpu.VMEM((32, width), f32),
            pltpu.VMEM((8, hidden), f32),
            pltpu.VMEM((width, width), bf16),
            pltpu.SemaphoreType.DMA,
        ],
        2 * tokens * width * (3 * width + 6 * hidden),
        tokens * width * 14,
        63,
    )(me, x, x_got, cot, cot_got, att, proj_weight, proj_bias[None], gain[None], shift[None], fc_weight, fc_bias[None],
      out_weight, out_bias[None])


def qkv_back_kernel(
    me_ref, x_ref, xg_ref, gain_ref, shift_ref, w_ref, dq_ref, dk_ref, dv_ref, gm_ref,
    kept_ref, sent_ref, dw_ref, small_ref, bias_ref, acc, sums, bias_sums,
):
    step = pl.program_id(0)
    steps = pl.num_programs(0)
    width = x_ref.shape[1]
    refs = (dq_ref, dk_ref, dv_ref)

    @pl.when(step == 0)
    def _():
        acc[...] = jnp.zeros_like(acc)
        sums[...] = jnp.zeros_like(sums)
        bias_sums[...] = jnp.zeros_like(bias_sums)

    hat, inverse = norm_parts(either(step, steps // 2, x_ref, xg_ref).astype(f32))
    normed_t = jnp.transpose((hat * gain_ref[...] + shift_ref[...]).astype(bf16))
    grad_t = sum(dot_nn(w_ref[:, i * width : (i + 1) * width], ref[...]) for i, ref in enumerate(refs))
    for i, ref in enumerate(refs):
        acc[i * width : (i + 1) * width, :] += dot_nt(normed_t, ref[...])
    grad_normed = jnp.transpose(grad_t)
    scaled = grad_normed * gain_ref[...]
    mean_one = jnp.mean(scaled, axis=-1, keepdims=True)
    mean_two = jnp.mean(scaled * hat, axis=-1, keepdims=True)
    grad_x = gm_ref[...].astype(f32) + inverse * (scaled - mean_one - hat * mean_two)
    sums[0:8, :] += row_sums(grad_normed * hat)
    sums[8:16, :] += row_sums(grad_normed)
    for i, ref in enumerate((dq_ref, dv_ref)):
        part = ref[...].astype(f32)
        bias_sums[i] += sum(part[:, j : j + 128] for j in range(0, part.shape[1], 128))

    @pl.when(step < steps // 2)
    def _():
        kept_ref[...] = grad_x

    @pl.when(step >= steps // 2)
    def _():
        sent_ref[...] = grad_x.astype(bf16)

    @pl.when(step == steps - 1)
    def _():
        dw_ref[...] = acc[...].astype(bf16)
        small_ref[...] = sums[...]
        bias_ref[...] = bias_sums[...]


def qkv_back(me, x, x_got, place, gain, shift, weight, dq, dk, dv, grad_middle):
    width, tokens = dq.shape
    own = pl.BlockSpec((TILE, width), place.own)
    got = pl.BlockSpec((TILE, width), place.got)
    turned = pl.BlockSpec((width, TILE), place.turned)
    return call(
        qkv_back_kernel,
        "qkv_backward",
        (place.steps,),
        [own, got, whole((1, width)), whole((1, width)), whole(weight.shape), turned, turned, turned,
         pl.BlockSpec((TILE, width), lambda t, me: (t, 0))],
        [own, got, whole((3 * width, width)), whole((16, width)), whole((2, width, 128))],
        [
            jax.ShapeDtypeStruct((tokens, width), f32),
            jax.ShapeDtypeStruct((tokens // 2, width), bf16),
            jax.ShapeDtypeStruct((3 * width, width), bf16),
            jax.ShapeDtypeStruct((16, width), f32),
            jax.ShapeDtypeStruct((2, width, 128), f32),
        ],
        [
            pltpu.VMEM((3 * width, width), f32),
            pltpu.VMEM((16, width), f32),
            pltpu.VMEM((2, width, 128), f32),
        ],
        4 * tokens * width * 3 * width,
        tokens * width * 20,
        62,
    )(me, x, x_got, gain[None], shift[None], weight, dq, dk, dv, grad_middle)


MESH = pl.DeviceIdType.MESH
PARTS = 6


def bits_of(rows):
    bits = [("rows", 1 << i) for i in range(rows.bit_length() - 1)]
    return bits[0], bits[1:] + [("seq", 1)], bits[2:] + bits[1:2] + [("seq", 1)]


def bit_value(bit):
    axis, weight = bit
    return lax.rem(lax.div(lax.axis_index(axis), weight), 2)


def partner(bit):
    axis, weight = bit
    return {axis: lax.axis_index(axis) + weight * (1 - 2 * bit_value(bit))}


def reduce_kernel(
    rows, one_ref, two_ref, small_ref, out_ref, two_out_ref, small_out_ref,
    buf, full, core_recv, recv, lines, line_recv, sems, core_sems, line_sems, local_sem,
):
    core, order_a, order_b = bits_of(rows)
    stages = len(order_a)
    total = buf.shape[0]
    part = total // 2 // PARTS
    orders = [order_b if p == 1 else order_a for p in range(PARTS)]

    barrier = pltpu.get_barrier_semaphore()
    for bit in [core] + order_a:
        pl.semaphore_signal(barrier, inc=1, device_id=partner(bit), device_id_type=MESH)
    split, depth = one_ref.shape[0], two_ref.shape[0]
    loads = [
        pltpu.make_async_copy(one_ref, buf.at[pl.ds(0, split)], local_sem.at[0]),
        pltpu.make_async_copy(two_ref, buf.at[pl.ds(split, depth)], local_sem.at[1]),
    ]
    for load in loads:
        load.start()
    lines[0] = small_ref[...]
    for load in loads:
        load.wait()
    pl.semaphore_wait(barrier, stages + 1)

    def ds(start, size):
        return pl.ds(pl.multiple_of(start, 16), size)

    def send(source, target, pair, bit):
        copy = pltpu.make_async_remote_copy(
            src_ref=source,
            dst_ref=target,
            send_sem=pair.at[0],
            recv_sem=pair.at[1],
            device_id=partner(bit),
            device_id_type=MESH,
        )
        copy.start()
        return copy

    line_bits = [core] + order_a

    def line_send(k):
        return send(lines.at[k], line_recv.at[k], line_sems.at[k], line_bits[k])

    def line_next(k, copy):
        copy.wait_recv()
        lines[k + 1] = lines[k] + line_recv[k]
        return copy

    sent = []
    mine = bit_value(core)
    copies = []
    for p in range(PARTS):
        other = (1 - mine) * (total // 2) + p * part
        copies.append(send(buf.at[ds(other, part)], core_recv.at[pl.ds(p * part, part)], core_sems.at[0, p], core))
    line = line_send(0)
    offsets = []
    for p in range(PARTS):
        copies[p].wait_recv()
        sent.append(copies[p])
        at = mine * (total // 2) + p * part
        offsets.append(at)
        buf[ds(at, part), :] = (
            buf[ds(at, part), :].astype(f32) + core_recv[p * part : (p + 1) * part, :].astype(f32)
        ).astype(bf16)
        copies[p] = None

    def halve(p, s):
        half = part >> (s + 1)
        bit = orders[p][s]
        value = bit_value(bit)
        base = part - (part >> s)
        copy = send(
            buf.at[ds(offsets[p] + (1 - value) * half, half)],
            recv.at[p, pl.ds(base, half)],
            sems.at[0, p, s],
            bit,
        )
        offsets[p] = offsets[p] + value * half
        return copy

    def settle(p, s, copy):
        half = part >> (s + 1)
        base = part - (part >> s)
        copy.wait_recv()
        sent.append(copy)
        rows_at = ds(offsets[p], half)
        total_now = buf[rows_at, :].astype(f32) + recv[p, base : base + half, :].astype(f32)
        return rows_at, total_now.astype(bf16)

    copies = [halve(p, 0) for p in range(PARTS)]
    line = line_next(0, line)
    sent.append(line)
    line = line_send(1)
    for s in range(1, stages):
        for p in range(PARTS):
            at, value = settle(p, s - 1, copies[p])
            buf[at, :] = value
            copies[p] = halve(p, s)
        line = line_next(s, line)
        sent.append(line)
        line = line_send(s + 1)

    def double(p, s):
        size = part >> (s + 1)
        bit = orders[p][s]
        at = ds(offsets[p], size)
        copy = send(full.at[at], full.at[at], sems.at[1, p, s], bit)
        offsets[p] = offsets[p] - bit_value(bit) * size
        return copy

    for p in range(PARTS):
        at, value = settle(p, stages - 1, copies[p])
        full[at, :] = value
        copies[p] = double(p, stages - 1)
    line = line_next(stages, line)
    sent.append(line)
    small_out_ref[...] = lines[stages + 1]
    for s in reversed(range(stages - 1)):
        for p in range(PARTS):
            copies[p].wait_recv()
            sent.append(copies[p])
            copies[p] = double(p, s)
    for p in range(PARTS):
        copies[p].wait_recv()
        sent.append(copies[p])
        at = ds(offsets[p], part)
        copies[p] = send(full.at[at], full.at[at], core_sems.at[1, p], core)
    for p in range(PARTS):
        copies[p].wait_recv()
        sent.append(copies[p])
    wide = full.shape[1]
    stores = []
    for i in range(total // depth):
        here = full.at[i * depth : (i + 1) * depth, :]
        there = out_ref.at[:, i * wide : (i + 1) * wide] if i * depth < split else two_out_ref
        stores.append(pltpu.make_async_copy(here, there, local_sem.at[2 + i]))
        stores[-1].start()
    for copy in sent:
        copy.wait_send()
    for store in stores:
        store.wait()


def sum_everywhere(one, two, small):
    rows = lax.axis_size("rows")
    depth, width = two.shape
    total = one.shape[0] + depth
    stages = len(bits_of(rows)[1])
    part = total // 2 // PARTS
    anywhere = pl.BlockSpec(memory_space=pl.ANY)
    vmem = pl.BlockSpec(memory_space=pltpu.VMEM)
    return pl.pallas_call(
        partial(reduce_kernel, rows),
        out_shape=[
            jax.ShapeDtypeStruct((depth, one.shape[0] // depth * width), bf16),
            jax.ShapeDtypeStruct(two.shape, bf16),
            jax.ShapeDtypeStruct(small.shape, f32),
        ],
        in_specs=[anywhere, anywhere, vmem],
        out_specs=[anywhere, anywhere, vmem],
        scratch_shapes=[
            pltpu.VMEM((total, width), bf16),
            pltpu.VMEM((total, width), bf16),
            pltpu.VMEM((total // 2, width), bf16),
            pltpu.VMEM((PARTS, part, width), bf16),
            pltpu.VMEM((stages + 2,) + small.shape, f32),
            pltpu.VMEM((stages + 1,) + small.shape, f32),
            pltpu.SemaphoreType.DMA((2, PARTS, stages, 2)),
            pltpu.SemaphoreType.DMA((2, PARTS, 2)),
            pltpu.SemaphoreType.DMA((stages + 1, 2)),
            pltpu.SemaphoreType.DMA((2 + total // depth,)),
        ],
        compiler_params=pltpu.CompilerParams(
            collective_id=0, has_side_effects=True, vmem_limit_bytes=40 * MIB
        ),
        cost_estimate=pl.CostEstimate(flops=total * width * 2, bytes_accessed=total * width * 4, transcendentals=0),
        name="sum_everywhere",
    )(one, two, small)


def place_kernel(me_ref, got_ref, _, out_ref):
    out_ref[...] = got_ref[...].astype(out_ref.dtype)


def put_in_place(me, got, target, place):
    width = got.shape[1]
    return call(
        place_kernel,
        "place_half",
        (place.phase,),
        [pl.BlockSpec((TILE, width), lambda t, me: (t, 0)), pl.BlockSpec(memory_space=pl.ANY)],
        pl.BlockSpec((TILE, width), place.back),
        jax.ShapeDtypeStruct(target.shape, target.dtype),
        [],
        0,
        got.size * 6,
        32,
        aliases={2: 0},
    )(me, got, target)


def swap(value):
    return lax.ppermute(value, "seq", [(0, 1), (1, 0)])


def after(value, *others):
    return lax.optimization_barrier((value,) + others)[0]


def row_local(
    block_input, segment_ids, norm1_gain, norm1_shift, qkv_weight, qv_bias, proj_weight, proj_bias,
    norm2_gain, norm2_shift, fc_weight, fc_bias, out_weight, out_bias, out_cotangent,
):
    held, half_len, width = block_input.shape
    rows, length = held // 2, 2 * half_len
    tokens = rows * length
    place = Place(rows, half_len)
    side = lax.axis_index("seq").astype(jnp.int32)
    first_side = side == 0

    def outgoing(value, row):
        return lax.dynamic_index_in_dim(value, row, 0, keepdims=False)

    me = side[None]
    left_rows = [(1 - side) * rows + r for r in range(rows)]
    x_out = outgoing(block_input, left_rows[0])
    x_parts = [swap(x_out)]
    mine = lax.dynamic_slice_in_dim(segment_ids, side * rows, rows, 0)
    other = swap(after(lax.dynamic_slice_in_dim(segment_ids, (1 - side) * rows, rows, 0), x_out))

    segments = jnp.concatenate((jnp.where(first_side, mine, other), jnp.where(first_side, other, mine)), axis=1)
    slot = jnp.arange(length, dtype=jnp.int32)[None]
    ends = [jnp.sum((segments <= doc).astype(jnp.int32), axis=1, keepdims=True) for doc in range(2)]
    start = jnp.where(
        segments == 0, 0, jnp.where(segments == 1, ends[0], jnp.where(segments == 2, ends[1], slot))
    )
    low = start[:, ::BLOCK] // BLOCK
    blocks = length // BLOCK
    high = jnp.sum((low[:, None, :] <= jnp.arange(blocks)[None, :, None]).astype(jnp.int32), axis=2) - 1
    start = start[:, None, :]
    low = low.reshape(-1)
    high = high.reshape(-1)

    x = block_input.reshape(held * half_len, width)
    cot = out_cotangent.reshape(held * half_len, width)
    bias = jnp.concatenate((qv_bias[:width], jnp.zeros((width,), f32), qv_bias[width:]))[:, None]
    params = (norm1_gain[None], norm1_shift[None], jnp.transpose(qkv_weight), bias)
    qkv = project_qkv(me, x, params, place, 0, place.phase, False, (), ())
    attended = ()
    for row in range(rows):
        if row + 1 < rows:
            x_parts.append(swap(after(outgoing(block_input, left_rows[row + 1]), x_parts[row], qkv[0])))
        qkv = project_qkv(
            me, x_parts[row], params, place, place.phase + row * place.per, place.per, True, qkv, attended[:1]
        )
        parts = 2 if row + 2 == rows else 1
        for part in range(parts):
            attended = attend(low, start, *qkv, row, length, part, parts, attended)
            if part + 1 < parts:
                cot_out = jnp.concatenate([outgoing(out_cotangent, left_rows[r]) for r in range(rows)], axis=0)
                cot_got = swap(after(cot_out, x_parts[row + 1], attended[1]))
    att, lse = attended
    x_got = jnp.concatenate(x_parts, axis=0)

    y, y_sent, grad_middle, grad_att, delta, dfc, dout, dproj, small_two, dfcb = feed_forward(
        me, x, x_got, cot, cot_got, att, place, proj_weight, proj_bias, norm2_gain, norm2_shift, fc_weight, fc_bias,
        out_weight, out_bias
    )
    dfc, dout = lax.psum((dfc, dout), ("rows", "seq"))
    y_got = swap(y_sent)
    dq, dk, dv = attend_back(high, start, *qkv, grad_att, lse, delta, rows)
    y = put_in_place(me, y_got, y, place)
    dq = after(dq, y)
    dx, dx_sent, dqkv, small_one, small_qv = qkv_back(
        me, x, x_got, place, norm1_gain, norm1_shift, qkv_weight, dq, dk, dv, grad_middle
    )
    dx_got = swap(dx_sent)
    small = jnp.sum(jnp.concatenate((small_two, small_one), axis=0).reshape(-1, 8, width), axis=1)
    small = jnp.concatenate(
        (small, jnp.sum(small_qv, axis=2), jnp.sum(dfcb, axis=0).reshape(-1, width)), axis=0
    )
    lines = small.shape[0]
    small = jnp.pad(small, ((0, -lines % 8), (0, 0)))
    dqkv, dproj, small = sum_everywhere(dqkv, dproj, small)
    layer_output = y.reshape(held, half_len, width)
    input_grad = put_in_place(me, dx_got, dx, place).reshape(held, half_len, width)

    return (
        layer_output,
        input_grad,
        small[4],
        small[5],
        dqkv.astype(f32),
        small[6:8].reshape(-1),
        dproj.astype(f32),
        small[3],
        small[0],
        small[1],
        dfc.astype(f32),
        small[8:lines].reshape(-1),
        dout.astype(f32),
        small[2],
    )


def solution(mesh):
    rows_spec = P("rows", "seq", None)
    in_specs = (rows_spec, P("rows", "seq")) + (P(),) * 12 + (rows_spec,)
    out_specs = (rows_spec, rows_spec) + (P(),) * 12
    body = row_local if mesh.shape["seq"] == 2 else local
    return jax.shard_map(body, mesh=mesh, in_specs=in_specs, out_specs=out_specs, check_vma=False)
```

profile of v0, /device:TPU:0, one launch (start us, length us, event | category | flops | bytes accessed | tf_op | source)
XLA Modules:
  0.0 671.6 jit_solution(4953446217091779223)
XLA Ops:
  7.3 3.8 dynamic-slice_bitcast_fusion.2
  11.0 3.0 collective-permute-start
  15.3 5.7 copy.48
  22.5 3.2 dynamic-slice_bitcast_fusion.1
  25.7 13.4 %qkv_forward.3 = (bf16[768,4096]{1,0:T(8,128)(2,1)}, bf16[768,4096]{1,0:T(8,128)(2,1)}, bf16[768,4096]{1,0:T(8,128)(2,1)}) custom-call(s32[1]{0:T(128)} %bitcast.me_ref, bf16[4096,768]{1,0:T(8,128)(2,1)} %bitcast.26, f32[1,768]{1,0:T(1,128)} %broadcast_in_dim.71.gain_ref, f32[1,768]{1,0:T(1,128)} %broadcast_in_dim.72.shift_ref, bf16[2304,768]{1,0:T(8,128)(2,1)} %bitcast.20, ...), custom_call_target="tpu_custom_call" | custom-call | flops 7247757312 | bytes 16121856 | tf_op jit(solution)/shard_map/qkv_forward/pallas_call | solution.py:497
  39.1 3.3 pad_maximum_fusion
  42.3 6.4 collective-permute-done.2
  52.3 8.4 %qkv_forward.4 = (bf16[768,4096]{1,0:T(8,128)(2,1)}, bf16[768,4096]{1,0:T(8,128)(2,1)}, bf16[768,4096]{1,0:T(8,128)(2,1)}) custom-call(s32[1]{0:T(128)} %bitcast.me_ref, bf16[1024,768]{1,0:T(8,128)(2,1)} %copy-done.4, f32[1,768]{1,0:T(1,128)} %broadcast_in_dim.71.gain_ref, ...), custom_call_target="tpu_custom_call", output_to_operand_aliasing={{0}: (6, {}), {1}: (7, {}), {2}: (8, {})} | custom-call | flops 3623878656 | bytes 9830400 | tf_op jit(solution)/shard_map/qkv_forward/pallas_call | solution.py:497
  60.7 15.2 %attention_forward.3 = (bf16[768,4096]{1,0:T(8,128)(2,1)}, f32[6,2,4096]{2,1,0:T(2,128)}) custom-call(s32[16]{0:T(128)} %reshape.194.low_ref, s32[2,1,2048]{2,1,0:T(1,128)} %compare_select_fusion.2.start_ref, bf16[768,4096]{1,0:T(8,128)(2,1)} %get-tuple-element.59.qt_ref.refs_0_, bf16[768,4096]{1,0:T(8,128)(2,1)} %get-tuple-element.60.kt_ref.refs_1_, ...), custom_call_target="tpu_custom_call" | custom-call | flops 1610612736 | bytes 12582912 | tf_op jit(solution)/shard_map/attention_forward/pallas_call | solution.py:613
  75.9 8.9 %collective-permute-done.1.x_ref = bf16[1024,768]{1,0:T(8,128)(2,1)S(1)} collective-permute-done((bf16[1024,768]{1,0:T(8,128)(2,1)}, bf16[1024,768]{1,0:T(8,128)(2,1)S(1)}, u32[]{:S(2)}, u32[]{:S(2)}) %collective-permute-start.1) | collective-permute-done | bytes 1572896 | tf_op jit(solution)/shard_map/ppermute | solution.py:1170
  91.8 17.2 %attention_forward.4 = (bf16[768,4096]{1,0:T(8,128)(2,1)}, f32[6,2,4096]{2,1,0:T(2,128)}) custom-call(s32[16]{0:T(128)} %reshape.194.low_ref, s32[2,1,2048]{2,1,0:T(1,128)} %compare_select_fusion.2.start_ref, bf16[768,4096]{1,0:T(8,128)(2,1)} %get-tuple-element.59.qt_ref.refs_0_, ...), custom_call_target="tpu_custom_call", output_to_operand_aliasing={{0}: (5, {}), {1}: (6, {})} | custom-call | flops 3221225472 | bytes 12582912 | tf_op jit(solution)/shard_map/attention_forward/pallas_call | solution.py:613
  109.0 8.4 %qkv_forward.5 = (bf16[768,4096]{1,0:T(8,128)(2,1)}, bf16[768,4096]{1,0:T(8,128)(2,1)}, bf16[768,4096]{1,0:T(8,128)(2,1)}) custom-call(s32[1]{0:T(128)} %bitcast.me_ref, bf16[1024,768]{1,0:T(8,128)(2,1)} %copy-done.3, f32[1,768]{1,0:T(1,128)} %broadcast_in_dim.71.gain_ref, ...), custom_call_target="tpu_custom_call", output_to_operand_aliasing={{0}: (6, {}), {1}: (7, {}), {2}: (8, {})} | custom-call | flops 3623878656 | bytes 9830400 | tf_op jit(solution)/shard_map/qkv_forward/pallas_call | solution.py:497
  117.4 37.3 %attention_forward.5 = (bf16[768,4096]{1,0:T(8,128)(2,1)}, f32[6,2,4096]{2,1,0:T(2,128)}) custom-call(s32[16]{0:T(128)} %reshape.194.low_ref, s32[2,1,2048]{2,1,0:T(1,128)} %compare_select_fusion.2.start_ref, bf16[768,4096]{1,0:T(8,128)(2,1)} %get-tuple-element.66.qt_ref, ...), custom_call_target="tpu_custom_call", output_to_operand_aliasing={{0}: (5, {}), {1}: (6, {})} | custom-call | flops 6442450944 | bytes 12582912 | tf_op jit(solution)/shard_map/attention_forward/pallas_call | solution.py:613
  154.8 192.6 %feed_forward.1 = (bf16[4096,768]{1,0:T(8,128)(2,1)}, bf16[2048,768]{1,0:T(8,128)(2,1)}, bf16[4096,768]{1,0:T(8,128)(2,1)}, bf16[768,4096]{1,0:T(8,128)(2,1)}, f...) custom-call(s32[1]{0:T(128)} %bitcast.me_ref, ...), custom_call_target="tpu_custom_call" | custom-call | flops 130459631616 | bytes 44040192 | tf_op jit(solution)/shard_map/feed_forward/pallas_call | solution.py:834
  348.1 97.0 %attention_backward.1 = (bf16[768,4096]{1,0:T(8,128)(2,1)}, bf16[768,4096]{1,0:T(8,128)(2,1)}, bf16[768,4096]{1,0:T(8,128)(2,1)}) custom-call(s32[16]{0:T(128)} %sub.17.high_ref, s32[2,1,2048]{2,1,0:T(1,128)} %compare_select_fusion.2.start_ref, bf16[768,4096]{1,0:T(8,128)(2,1)} %get-tuple-element.66.qt_ref, bf16[768,4096]{1,0:T(8,128)(2,1)} %get-tuple-element.67.kt_ref, ...), custom_call_target="tpu_custom_call" | custom-call | flops 32212254720 | bytes 44040192 | tf_op jit(solution)/shard_map/attention_backward/pallas_call | solution.py:712
  445.1 4.2 place_half.2
  449.3 45.6 %qkv_backward.1 = (f32[4096,768]{1,0:T(8,128)}, bf16[2048,768]{1,0:T(8,128)(2,1)}, bf16[2304,768]{1,0:T(8,128)(2,1)}, f32[16,768]{1,0:T(8,128)}, f32[2,768,128]{2,1,0:T(8,128)}) custom-call(s32[1]{0:T(128)} %bitcast.me_ref, bf16[4096,768]{1,0:T(8,128)(2,1)} %bitcast.28, bf16[2048,768]{1,0:T(8,128)(2,1)} %constant_dynamic-update-slice_fusion.xg_ref, ...), custom_call_target="tpu_custom_call" | custom-call | flops 28991029248 | bytes 62914560 | tf_op jit(solution)/shard_map/qkv_backward/pallas_call | solution.py:922
  497.4 2.0 copy-done
  500.7 139.4 %sum_everywhere.1 = (bf16[768,2304]{1,0:T(8,128)(2,1)S(1)}, bf16[768,768]{1,0:T(8,128)(2,1)S(1)}, f32[16,768]{1,0:T(8,128)S(1)}) custom-call(bf16[2304,768]{1,0:T(8,128)(2,1)S(1)} %copy-done, bf16[768,768]{1,0:T(8,128)(2,1)S(1)} %copy-done.2, f32[16,768]{1,0:T(8,128)S(1)} %select_maximum_fusion.small_ref), custom_call_target="tpu_custom_call" | custom-call | flops 4718592 | bytes 9437184 | tf_op jit(solution)/shard_map/sum_everywhere/pallas_call | solution.py:1119
  641.1 3.5 convert_element_type.26
  645.2 2.8 convert_element_type.27
  649.3 7.5 %convert_element_type.28 = f32[768,3072]{1,0:T(8,128)} convert(bf16[768,3072]{1,0:T(8,128)(2,1)} %get-tuple-element.102) | non-fusion elementwise | flops 2359296 | bytes 14155776 | tf_op jit(solution)/shard_map/convert_element_type | solution.py:1266
  656.8 4.5 convert_element_type.29
  661.3 3.0 place_half.3
  (82 shorter events, 20.5 us)
Async XLA Ops:
  7.2 6.8 %copy-start.9 = (s32[4,1024]{1,0:T(4,128)S(1)}, s32[4,1024]{1,0:T(4,128)}, u32[]{:S(2)}) copy-start(s32[4,1024]{1,0:T(4,128)} %param.16) | copy-start | bytes 49156
  7.2 6.9 %copy-start.10 = (f32[1536]{0:T(1024)S(1)}, f32[1536]{0:T(1024)}, u32[]{:S(2)}) copy-start(f32[1536]{0:T(1024)} %param.20) | copy-start | bytes 18436
  7.2 6.9 %copy-start.11 = (f32[768]{0:T(1024)S(1)}, f32[768]{0:T(1024)}, u32[]{:S(2)}) copy-start(f32[768]{0:T(1024)} %param.17) | copy-start | bytes 9220
  7.2 7.5 %copy-start.12 = (f32[768]{0:T(1024)S(1)}, f32[768]{0:T(1024)}, u32[]{:S(2)}) copy-start(f32[768]{0:T(1024)} %param.18) | copy-start | bytes 9220
  7.2 642.1 %all-reduce.4.cloned.1.call-start = ((), (), s32[]{:S(2)}) async-start(), calls=%async_computation | async-start | bytes 18874368 | tf_op jit(solution)/shard_map/psum | solution.py:1236
  11.0 37.9 %collective-permute-start = (bf16[1024,768]{1,0:T(8,128)(2,1)}, bf16[1024,768]{1,0:T(8,128)(2,1)S(1)}, u32[]{:S(2)}, u32[]{:S(2)}) collective-permute-start(bf16[1024,768]{1,0:T(8,128)(2,1)} %get-tuple-element.107), channel_id=1, source_target_pairs={{0,1},{1,0},{2,3},{3,2},{4,5},{5,4},{6,7},{7,6},{8,9},{9,8},{10,11... | collective-permute-start | bytes 4718600 | tf_op jit(solution)/shard_map/ppermute | solution.py:1170
  14.0 34.8 %collective-permute-start.2 = (s32[2,1024]{1,0:T(2,128)S(1)}, s32[2,1024]{1,0:T(2,128)S(1)}, u32[]{:S(2)}, u32[]{:S(2)}) collective-permute-start(s32[2,1024]{1,0:T(2,128)S(1)} %constant_dynamic-slice_fusion), channel_id=1, source_target_pairs={{0,1},{1,0},{2,3},{3,2},{4,5},{5,4},{6,7},{7,6},{8,9},{9,8},{10,11... | collective-permute-start | bytes 24584 | tf_op jit(solution)/shard_map/ppermute | solution.py:1170
  49.0 3.3 copy-start.4
  49.0 35.9 %collective-permute-start.1 = (bf16[1024,768]{1,0:T(8,128)(2,1)}, bf16[1024,768]{1,0:T(8,128)(2,1)S(1)}, u32[]{:S(2)}, u32[]{:S(2)}) collective-permute-start(bf16[1024,768]{1,0:T(8,128)(2,1)} %get-tuple-element.55), channel_id=1, source_target_pairs={{0,1},{1,0},{2,3},{3,2},{4,5},{5,4},{6,7},{7,6},{8,9},{9,8},{10,11... | collective-permute-start | bytes 4718600 | tf_op jit(solution)/shard_map/ppermute | solution.py:1170
  60.7 25.6 %copy-start.13 = (f32[768]{0:T(1024)S(1)}, f32[768]{0:T(1024)}, u32[]{:S(2)}) copy-start(f32[768]{0:T(1024)} %param.22) | copy-start | bytes 9220
  60.7 26.1 %copy-start.14 = (f32[768]{0:T(1024)S(1)}, f32[768]{0:T(1024)}, u32[]{:S(2)}) copy-start(f32[768]{0:T(1024)} %param.23) | copy-start | bytes 9220
  60.7 26.7 %copy-start.15 = (f32[768]{0:T(1024)S(1)}, f32[768]{0:T(1024)}, u32[]{:S(2)}) copy-start(f32[768]{0:T(1024)} %param.24) | copy-start | bytes 9220
  60.7 27.3 %copy-start.16 = (f32[768]{0:T(1024)S(1)}, f32[768]{0:T(1024)}, u32[]{:S(2)}) copy-start(f32[768]{0:T(1024)} %param.28) | copy-start | bytes 9220
  60.7 28.6 %copy-start.5 = (bf16[1024,768]{1,0:T(8,128)(2,1)S(1)}, bf16[1024,768]{1,0:T(8,128)(2,1)}, u32[]{:S(2)}) copy-start(bf16[1024,768]{1,0:T(8,128)(2,1)} %copy-done.4) | copy-start | bytes 4718596
  84.8 24.1 %copy-start.3 = (bf16[1024,768]{1,0:T(8,128)(2,1)}, bf16[1024,768]{1,0:T(8,128)(2,1)S(1)}, u32[]{:S(2)}) copy-start(bf16[1024,768]{1,0:T(8,128)(2,1)S(1)} %collective-permute-done.1.x_ref) | copy-start | bytes 4718596
  84.8 69.9 %collective-permute-start.3 = (bf16[2048,768]{1,0:T(8,128)(2,1)}, bf16[2048,768]{1,0:T(8,128)(2,1)}, u32[]{:S(2)}, u32[]{:S(2)}) collective-permute-start(bf16[2048,768]{1,0:T(8,128)(2,1)} %pad_maximum_fusion), channel_id=1, source_target_pairs={{0,1},{1,0},{2,3},{3,2},{4,5},{5,4},{6,7},{7,6},{8,9},{9,8},{10,11... | collective-permute-start | bytes 9437192 | tf_op jit(solution)/shard_map/ppermute | solution.py:1170
  154.8 192.7 %copy-start.17 = (s32[2,8]{1,0:T(2,128)S(1)}, s32[2,8]{1,0:T(2,128)}, u32[]{:S(2)}) copy-start(s32[2,8]{1,0:T(2,128)} %convert_reduce_fusion) | copy-start | bytes 196
  347.3 97.7 %collective-permute-start.4 = (bf16[2048,768]{1,0:T(8,128)(2,1)}, bf16[2048,768]{1,0:T(8,128)(2,1)}, u32[]{:S(2)}, u32[]{:S(2)}) collective-permute-start(bf16[2048,768]{1,0:T(8,128)(2,1)} %get-tuple-element.71), channel_id=1, source_target_pairs={{0,1},{1,0},{2,3},{3,2},{4,5},{5,4},{6,7},{7,6},{8,9},{9,8},{10,11... | collective-permute-start | bytes 9437192 | tf_op jit(solution)/shard_map/ppermute | solution.py:1170
  449.3 45.7 %copy-start.7 = (f32[8,3072]{1,0:T(8,128)S(1)}, f32[8,3072]{1,0:T(8,128)}, u32[]{:S(2)}) copy-start(f32[8,3072]{1,0:T(8,128)} %get-tuple-element.88) | copy-start | bytes 294916
  449.3 47.2 %copy-start.8 = (f32[32,768]{1,0:T(8,128)S(1)}, f32[32,768]{1,0:T(8,128)}, u32[]{:S(2)}) copy-start(f32[32,768]{1,0:T(8,128)} %get-tuple-element.85) | copy-start | bytes 294916
  494.9 166.4 %collective-permute-start.5 = (bf16[2048,768]{1,0:T(8,128)(2,1)}, bf16[2048,768]{1,0:T(8,128)(2,1)S(1)}, u32[]{:S(2)}, u32[]{:S(2)}) collective-permute-start(bf16[2048,768]{1,0:T(8,128)(2,1)} %get-tuple-element.81), channel_id=1, source_target_pairs={{0,1},{1,0},{2,3},{3,2},{4,5},{5,4},{6,7},{7,6},{8,9},{9,8},{10,11... | collective-permute-start | bytes 9437192 | tf_op jit(solution)/shard_map/ppermute | solution.py:1170
  497.4 2.1 copy-start
  499.4 1.3 copy-start.2
  649.3 7.5 %copy-start.6 = (bf16[3072,768]{1,0:T(8,128)(2,1)S(1)}, bf16[3072,768]{1,0:T(8,128)(2,1)}, u32[]{:S(2)}) copy-start(bf16[3072,768]{1,0:T(8,128)(2,1)} %get-tuple-element.103) | copy-start | bytes 14155780
  (1 other events, 1.0 us)
Sparse Core Ops, SparseCore 0:
  348.2 248.9 all-reduce.3
where the time goes:
time: 681 us; the launch traced here: 672 us
  Pallas kernels  582 us (85%)
  local copies, waits for them, and re-layouts  27.7 us (4%)
  other arithmetic  25.6 us (4%)
  waiting for transfers between devices  15.3 us (2%)
  between operations  14.8 us (2%)
    pallas_call x1, Pallas kernels, feed_forward(): call(mlp_kernel, 'feed_forward', (place.steps,), [own, got, own, got, tur...  193 us
    pallas_call x1, Pallas kernels, sum_everywhere(): pl.pallas_call(partial(reduce_kernel, rows), out_shape=[jax.ShapeDtypeStr...  139 us
    pallas_call x1, Pallas kernels, attend_back(): call(attend_back_kernel, 'attention_backward', (rows,), [pl.BlockSpec((1,...  97 us
    pallas_call x3, Pallas kernels, attend(): call(partial(attend_kernel, row=row, first=part * span // BLOCK, blocks=l...  69.7 us
    pallas_call x1, Pallas kernels, qkv_back(): call(qkv_back_kernel, 'qkv_backward', (place.steps,), [own, got, whole((1...  45.6 us
    pallas_call x3, Pallas kernels, project_qkv(): call(qkv_kernel, 'qkv_forward', (count,), [pl.BlockSpec((TILE, width), in...  30.2 us
    ppermute x6, waiting for transfers between devices, swap(): return lax.ppermute(value, 'seq', [(0, 1), (1, 0)])  15.3 us
  transfers between devices with their start and end apart: 7, of which 2 were waited for; matrix products, arithmetic and copies ran while one was open for 7% of the time, Pallas kernels for 57%

commit v1 on v0

--- a/solution.py
+++ b/solution.py
@@ -732,14 +732,14 @@
     me_ref, x_ref, xg_ref, cot_ref, cotg_ref, att_ref, proj_ref, projb_ref, gain_ref, shift_ref, fc_ref, fcb_ref,
     out_ref, outb_ref,
     kept_ref, sent_ref, gm_ref, do_ref, delta_ref, dfc_ref, dout_ref, dproj_ref, small_ref, dfcb_ref,
-    dfc, doutt, dproj, sums, dfcb, stage, sem,
+    dfc, doutt, dproj, sums, dfcb, stage, stage_t, sem,
 ):
     step = pl.program_id(0)
     steps = pl.num_programs(0)
     phase = steps // 2
     tile, width = x_ref.shape
     hidden = fc_ref.shape[1]
-    chunk = 768
+    chunk = width
 
     @pl.when(step == 0)
     def _():
@@ -777,14 +777,6 @@
         dfcb[:, cols] += row_sums(grad_pre.astype(f32))
     y = (middle + BRANCH * (branch + outb_ref[...])).astype(bf16)
 
-    @pl.when(step < phase)
-    def _():
-        kept_ref[...] = y
-
-    @pl.when(step >= phase)
-    def _():
-        sent_ref[...] = y
-
     scaled = grad_normed * gain_ref[...]
     mean_one = jnp.mean(scaled, axis=-1, keepdims=True)
     mean_two = jnp.mean(scaled * hat, axis=-1, keepdims=True)
@@ -803,17 +795,31 @@
     sums[16:24, :] += row_sums(grad_two.astype(f32))
     sums[24:32, :] += row_sums(grad_one.astype(f32))
 
+    @pl.when(step < phase)
+    def _():
+        kept_ref[...] = y
+
+    @pl.when(step >= phase)
+    def _():
+        sent_ref[...] = y
+
     @pl.when(step == steps - 1)
     def _():
-        for at in range(0, hidden, chunk):
-            cols = slice(at, at + chunk)
+        copies = []
+        piece = stage_t.shape[0]
+        for i, at in enumerate(range(0, hidden, piece)):
+            cols = slice(at, at + piece)
+            if i > 0:
+                copies[-2].wait()
             stage[...] = dfc[:, cols].astype(bf16)
-            copy = pltpu.make_async_copy(stage, dfc_ref.at[:, cols], sem)
-            copy.start()
-            copy.wait()
-            stage[...] = jnp.transpose(doutt[:, cols].astype(bf16))
-            copy = pltpu.make_async_copy(stage, dout_ref.at[cols, :], sem)
-            copy.start()
+            copies.append(pltpu.make_async_copy(stage, dfc_ref.at[:, cols], sem.at[0]))
+            copies[-1].start()
+            if i > 0:
+                copies[-2].wait()
+            stage_t[...] = jnp.transpose(doutt[:, cols].astype(bf16))
+            copies.append(pltpu.make_async_copy(stage_t, dout_ref.at[cols, :], sem.at[1]))
+            copies[-1].start()
+        for copy in copies[-2:]:
             copy.wait()
         dproj_ref[...] = dproj[...].astype(bf16)
         small_ref[...] = sums[...]
@@ -858,8 +864,9 @@
             pltpu.VMEM((width, width), f32),
             pltpu.VMEM((32, width), f32),
             pltpu.VMEM((8, hidden), f32),
-            pltpu.VMEM((width, width), bf16),
-            pltpu.SemaphoreType.DMA,
+            pltpu.VMEM((width, width // 2), bf16),
+            pltpu.VMEM((width // 2, width), bf16),
+            pltpu.SemaphoreType.DMA((2,)),
         ],
         2 * tokens * width * (3 * width + 6 * hidden),
         tokens * width * 14,
@@ -964,7 +971,7 @@
 
 
 def reduce_kernel(
-    rows, one_ref, two_ref, small_ref, out_ref, two_out_ref, small_out_ref,
+    rows, one_ref, two_ref, second_ref, first_ref, qv_ref, hidden_ref, out_ref, two_out_ref, small_out_ref,
     buf, full, core_recv, recv, lines, line_recv, sems, core_sems, line_sems, local_sem,
 ):
     core, order_a, order_b = bits_of(rows)
@@ -983,7 +990,14 @@
     ]
     for load in loads:
         load.start()
-    lines[0] = small_ref[...]
+    width = buf.shape[1]
+    values = [second_ref[i : i + 8, :] for i in range(0, second_ref.shape[0], 8)]
+    values += [first_ref[i : i + 8, :] for i in range(0, first_ref.shape[0], 8)]
+    values += [jnp.transpose(qv_ref[i]) for i in range(qv_ref.shape[0])]
+    values += [hidden_ref[:, i : i + width] for i in range(0, hidden_ref.shape[1], width)]
+    lines[0] = jnp.zeros(lines.shape[1:], f32)
+    for i, value in enumerate(values):
+        lines[0, i : i + 1, :] = jnp.sum(value, axis=0, keepdims=True)
     for load in loads:
         load.wait()
     pl.semaphore_wait(barrier, stages + 1)
@@ -1108,12 +1122,14 @@
         store.wait()
 
 
-def sum_everywhere(one, two, small):
+def sum_everywhere(one, two, second, first, qv, hidden):
     rows = lax.axis_size("rows")
     depth, width = two.shape
     total = one.shape[0] + depth
     stages = len(bits_of(rows)[1])
     part = total // 2 // PARTS
+    count = (second.shape[0] + first.shape[0] + hidden.size // width) // 8 + qv.shape[0]
+    small = jax.ShapeDtypeStruct((count + -count % 8, width), f32)
     anywhere = pl.BlockSpec(memory_space=pl.ANY)
     vmem = pl.BlockSpec(memory_space=pltpu.VMEM)
     return pl.pallas_call(
@@ -1121,9 +1137,9 @@
         out_shape=[
             jax.ShapeDtypeStruct((depth, one.shape[0] // depth * width), bf16),
             jax.ShapeDtypeStruct(two.shape, bf16),
-            jax.ShapeDtypeStruct(small.shape, f32),
+            small,
         ],
-        in_specs=[anywhere, anywhere, vmem],
+        in_specs=[anywhere, anywhere, vmem, vmem, vmem, vmem],
         out_specs=[anywhere, anywhere, vmem],
         scratch_shapes=[
             pltpu.VMEM((total, width), bf16),
@@ -1138,11 +1154,11 @@
             pltpu.SemaphoreType.DMA((2 + total // depth,)),
         ],
         compiler_params=pltpu.CompilerParams(
-            collective_id=0, has_side_effects=True, vmem_limit_bytes=40 * MIB
+            collective_id=0, has_side_effects=True, vmem_limit_bytes=60 * MIB
         ),
         cost_estimate=pl.CostEstimate(flops=total * width * 2, bytes_accessed=total * width * 4, transcendentals=0),
         name="sum_everywhere",
-    )(one, two, small)
+    )(one, two, second, first, qv, hidden)
 
 
 def place_kernel(me_ref, got_ref, _, out_ref):
@@ -1224,8 +1240,8 @@
         for part in range(parts):
             attended = attend(low, start, *qkv, row, length, part, parts, attended)
             if part + 1 < parts:
-                cot_out = jnp.concatenate([outgoing(out_cotangent, left_rows[r]) for r in range(rows)], axis=0)
-                cot_got = swap(after(cot_out, x_parts[row + 1], attended[1]))
+                cot_out = lax.dynamic_slice_in_dim(out_cotangent, left_rows[0], rows, 0)
+                cot_got = swap(after(cot_out, x_parts[row + 1], attended[1])).reshape(tokens // 2, width)
     att, lse = attended
     x_got = jnp.concatenate(x_parts, axis=0)
 
@@ -1242,13 +1258,7 @@
         me, x, x_got, place, norm1_gain, norm1_shift, qkv_weight, dq, dk, dv, grad_middle
     )
     dx_got = swap(dx_sent)
-    small = jnp.sum(jnp.concatenate((small_two, small_one), axis=0).reshape(-1, 8, width), axis=1)
-    small = jnp.concatenate(
-        (small, jnp.sum(small_qv, axis=2), jnp.sum(dfcb, axis=0).reshape(-1, width)), axis=0
-    )
-    lines = small.shape[0]
-    small = jnp.pad(small, ((0, -lines % 8), (0, 0)))
-    dqkv, dproj, small = sum_everywhere(dqkv, dproj, small)
+    dqkv, dproj, small = sum_everywhere(dqkv, dproj, small_two, small_one, small_qv, dfcb)
     layer_output = y.reshape(held, half_len, width)
     input_grad = put_in_place(me, dx_got, dx, place).reshape(held, half_len, width)
 
@@ -1264,7 +1274,7 @@
         small[0],
         small[1],
         dfc.astype(f32),
-        small[8:lines].reshape(-1),
+        small[8 : 8 + dfcb.shape[1] // width].reshape(-1),
         dout.astype(f32),
         small[2],
     )

time: 681 us -> 669 us (0.982)
  Pallas kernels: 582 us -> 554 us
  waiting for transfers between devices: 15.3 us -> 40.2 us
    ppermute x6, waiting for transfers between devices: 15.3 us -> 40.2 us  [swap(): return lax.ppermute(value, 'seq', [(0, 1), (1, 0)])]
    pallas_call x1, Pallas kernels: 97 us -> 80 us  [attend_back(): call(attend_back_kernel, 'attention_backward', (rows,), [pl.BlockSpec((1,...]
    pallas_call x3, Pallas kernels: 69.7 us -> 60 us  [attend(): call(partial(attend_kernel, row=row, first=part * span // BLOCK, blocks=l...]
    pallas_call x1, Pallas kernels: 193 us -> 184 us  [feed_forward(): call(mlp_kernel, 'feed_forward', (place.steps,), [own, got, own, got, tur...]
  transfers between devices with their start and end apart: 7 -> 7, of which waited for: 2 -> 4; matrix products, arithmetic and copies ran while one was open for 7% -> 7% of each run, Pallas kernels for 57% -> 55%
where the time goes in v1:
time: 669 us; the launch traced here: 666 us
  Pallas kernels  554 us (83%)
  waiting for transfers between devices  40.2 us (6%)
  local copies, waits for them, and re-layouts  25.8 us (4%)
  other arithmetic  22 us (3%)
  between operations  14.6 us (2%)
  starting transfers between devices  9.3 us (1%)
    pallas_call x1, Pallas kernels, feed_forward(): call(mlp_kernel, 'feed_forward', (place.steps,), [own, got, own, got, tur...  184 us
    pallas_call x1, Pallas kernels, sum_everywhere(): pl.pallas_call(partial(reduce_kernel, rows), out_shape=[jax.ShapeDtypeStr...  146 us
    pallas_call x1, Pallas kernels, attend_back(): call(attend_back_kernel, 'attention_backward', (rows,), [pl.BlockSpec((1,...  80 us
    pallas_call x3, Pallas kernels, attend(): call(partial(attend_kernel, row=row, first=part * span // BLOCK, blocks=l...  60 us
    pallas_call x1, Pallas kernels, qkv_back(): call(qkv_back_kernel, 'qkv_backward', (place.steps,), [own, got, whole((1...  45.9 us
    ppermute x6, waiting for transfers between devices, swap(): return lax.ppermute(value, 'seq', [(0, 1), (1, 0)])  40.2 us
    pallas_call x3, Pallas kernels, project_qkv(): call(qkv_kernel, 'qkv_forward', (count,), [pl.BlockSpec((TILE, width), in...  30.5 us
  transfers between devices with their start and end apart: 7, of which 4 were waited for; matrix products, arithmetic and copies ran while one was open for 7% of the time, Pallas kernels for 55%

profile of v1, /device:TPU:0, one launch (start us, length us, event | category | flops | bytes accessed | tf_op | source)
XLA Modules:
  0.0 665.6 jit_solution(6228909712514805854)
XLA Ops:
  7.3 3.2 dynamic-slice_bitcast_fusion
  10.5 3.0 collective-permute-start
  14.7 5.7 copy.48
  21.9 13.4 %qkv_forward.3 = (bf16[768,4096]{1,0:T(8,128)(2,1)}, bf16[768,4096]{1,0:T(8,128)(2,1)}, bf16[768,4096]{1,0:T(8,128)(2,1)}) custom-call(s32[1]{0:T(128)} %bitcast.me_ref, bf16[4096,768]{1,0:T(8,128)(2,1)} %bitcast.19, f32[1,768]{1,0:T(1,128)} %broadcast_in_dim.71.gain_ref, f32[1,768]{1,0:T(1,128)} %broadcast_in_dim.72.shift_ref, bf16[2304,768]{1,0:T(8,128)(2,1)} %bitcast.13, ...), custom_call_target="tpu_custom_call" | custom-call | flops 7247757312 | bytes 16121856 | tf_op jit(solution)/shard_map/qkv_forward/pallas_call | solution.py:497
  35.3 3.7 constant_dynamic-slice_fusion.1
  39.0 9.0 %collective-permute-done.2 = s32[2,1024]{1,0:T(2,128)S(1)} collective-permute-done((s32[2,1024]{1,0:T(2,128)S(1)}, s32[2,1024]{1,0:T(2,128)S(1)}, u32[]{:S(2)}, u32[]{:S(2)}) %collective-permute-start.2) | collective-permute-done | bytes 8224 | tf_op jit(solution)/shard_map/ppermute | solution.py:1186
  51.6 8.4 %qkv_forward.4 = (bf16[768,4096]{1,0:T(8,128)(2,1)}, bf16[768,4096]{1,0:T(8,128)(2,1)}, bf16[768,4096]{1,0:T(8,128)(2,1)}) custom-call(s32[1]{0:T(128)} %bitcast.me_ref, bf16[1024,768]{1,0:T(8,128)(2,1)} %copy-done.1, f32[1,768]{1,0:T(1,128)} %broadcast_in_dim.71.gain_ref, ...), custom_call_target="tpu_custom_call", output_to_operand_aliasing={{0}: (6, {}), {1}: (7, {}), {2}: (8, {})} | custom-call | flops 3623878656 | bytes 9830400 | tf_op jit(solution)/shard_map/qkv_forward/pallas_call | solution.py:497
  60.0 13.3 %attention_forward.3 = (bf16[768,4096]{1,0:T(8,128)(2,1)}, f32[6,2,4096]{2,1,0:T(2,128)}) custom-call(s32[16]{0:T(128)} %reshape.191.low_ref, s32[2,1,2048]{2,1,0:T(1,128)} %compare_select_fusion.2.start_ref, bf16[768,4096]{1,0:T(8,128)(2,1)} %get-tuple-element.59.qt_ref.refs_0_, bf16[768,4096]{1,0:T(8,128)(2,1)} %get-tuple-element.60.kt_ref.refs_1_, ...), custom_call_target="tpu_custom_call" | custom-call | flops 1610612736 | bytes 12582912 | tf_op jit(solution)/shard_map/attention_forward/pallas_call | solution.py:613
  73.3 10.8 %collective-permute-done.1.x_ref = bf16[1024,768]{1,0:T(8,128)(2,1)S(1)} collective-permute-done((bf16[1024,768]{1,0:T(8,128)(2,1)}, bf16[1024,768]{1,0:T(8,128)(2,1)S(1)}, u32[]{:S(2)}, u32[]{:S(2)}) %collective-permute-start.1) | collective-permute-done | bytes 1572896 | tf_op jit(solution)/shard_map/ppermute | solution.py:1186
  91.0 23.5 %attention_forward.4 = (bf16[768,4096]{1,0:T(8,128)(2,1)}, f32[6,2,4096]{2,1,0:T(2,128)}) custom-call(s32[16]{0:T(128)} %reshape.191.low_ref, s32[2,1,2048]{2,1,0:T(1,128)} %compare_select_fusion.2.start_ref, bf16[768,4096]{1,0:T(8,128)(2,1)} %get-tuple-element.59.qt_ref.refs_0_, ...), custom_call_target="tpu_custom_call", output_to_operand_aliasing={{0}: (5, {}), {1}: (6, {})} | custom-call | flops 3221225472 | bytes 12582912 | tf_op jit(solution)/shard_map/attention_forward/pallas_call | solution.py:613
  114.6 8.7 %qkv_forward.5 = (bf16[768,4096]{1,0:T(8,128)(2,1)}, bf16[768,4096]{1,0:T(8,128)(2,1)}, bf16[768,4096]{1,0:T(8,128)(2,1)}) custom-call(s32[1]{0:T(128)} %bitcast.me_ref, bf16[1024,768]{1,0:T(8,128)(2,1)} %copy-done, f32[1,768]{1,0:T(1,128)} %broadcast_in_dim.71.gain_ref, ...), custom_call_target="tpu_custom_call", output_to_operand_aliasing={{0}: (6, {}), {1}: (7, {}), {2}: (8, {})} | custom-call | flops 3623878656 | bytes 9830400 | tf_op jit(solution)/shard_map/qkv_forward/pallas_call | solution.py:497
  123.3 23.2 %attention_forward.5 = (bf16[768,4096]{1,0:T(8,128)(2,1)}, f32[6,2,4096]{2,1,0:T(2,128)}) custom-call(s32[16]{0:T(128)} %reshape.191.low_ref, s32[2,1,2048]{2,1,0:T(1,128)} %compare_select_fusion.2.start_ref, bf16[768,4096]{1,0:T(8,128)(2,1)} %get-tuple-element.66.qt_ref, ...), custom_call_target="tpu_custom_call", output_to_operand_aliasing={{0}: (5, {}), {1}: (6, {})} | custom-call | flops 6442450944 | bytes 12582912 | tf_op jit(solution)/shard_map/attention_forward/pallas_call | solution.py:613
  146.5 6.3 collective-permute-done.3
  152.8 184.3 %feed_forward.1 = (bf16[4096,768]{1,0:T(8,128)(2,1)}, bf16[2048,768]{1,0:T(8,128)(2,1)}, bf16[4096,768]{1,0:T(8,128)(2,1)}, bf16[768,4096]{1,0:T(8,128)(2,1)}, f...) custom-call(s32[1]{0:T(128)} %bitcast.me_ref, ...), custom_call_target="tpu_custom_call" | custom-call | flops 130459631616 | bytes 44040192 | tf_op jit(solution)/shard_map/feed_forward/pallas_call | solution.py:840
  338.9 80.0 %attention_backward.1 = (bf16[768,4096]{1,0:T(8,128)(2,1)}, bf16[768,4096]{1,0:T(8,128)(2,1)}, bf16[768,4096]{1,0:T(8,128)(2,1)}) custom-call(s32[16]{0:T(128)} %sub.17.high_ref, s32[2,1,2048]{2,1,0:T(1,128)} %compare_select_fusion.2.start_ref, bf16[768,4096]{1,0:T(8,128)(2,1)} %get-tuple-element.66.qt_ref, bf16[768,4096]{1,0:T(8,128)(2,1)} %get-tuple-element.67.kt_ref, ...), custom_call_target="tpu_custom_call" | custom-call | flops 32212254720 | bytes 44040192 | tf_op jit(solution)/shard_map/attention_backward/pallas_call | solution.py:712
  418.8 14.1 %collective-permute-done.4.got_ref = bf16[2048,768]{1,0:T(8,128)(2,1)} collective-permute-done((bf16[2048,768]{1,0:T(8,128)(2,1)}, bf16[2048,768]{1,0:T(8,128)(2,1)}, u32[]{:S(2)}, u32[]{:S(2)}) %collective-permute-start.4) | collective-permute-done | bytes 3145760 | tf_op jit(solution)/shard_map/ppermute | solution.py:1186
  432.9 4.2 place_half.2
  437.1 45.9 %qkv_backward.1 = (f32[4096,768]{1,0:T(8,128)}, bf16[2048,768]{1,0:T(8,128)(2,1)}, bf16[2304,768]{1,0:T(8,128)(2,1)}, f32[16,768]{1,0:T(8,128)}, f32[2,768,128]{2,1,0:T(8,128)}) custom-call(s32[1]{0:T(128)} %bitcast.me_ref, bf16[4096,768]{1,0:T(8,128)(2,1)} %bitcast.21, bf16[2048,768]{1,0:T(8,128)(2,1)} %constant_dynamic-update-slice_fusion.xg_ref, ...), custom_call_target="tpu_custom_call" | custom-call | flops 28991029248 | bytes 62914560 | tf_op jit(solution)/shard_map/qkv_backward/pallas_call | solution.py:929
  484.9 145.7 %sum_everywhere.1 = (bf16[768,2304]{1,0:T(8,128)(2,1)}, bf16[768,768]{1,0:T(8,128)(2,1)}, f32[16,768]{1,0:T(8,128)}) custom-call(bf16[2304,768]{1,0:T(8,128)(2,1)} %get-tuple-element.83.one_ref, bf16[768,768]{1,0:T(8,128)(2,1)} %get-tuple-element.84.two_ref, f32[32,768]{1,0:T(8,128)} %get-tuple-element.85.second_ref, f32[16,768]{1,0:T(8,128)} %get-tuple-element.86.first_ref, ...), custom_call_target="tpu_custom_call" | custom-call | flops 4718592 | bytes 9437184 | tf_op jit(solution)/shard_map/sum_everywhere/pallas_call | solution.py:1135
  632.1 5.5 convert_element_type.24
  638.2 2.8 convert_element_type.25
  643.3 7.5 %convert_element_type.26 = f32[768,3072]{1,0:T(8,128)} convert(bf16[768,3072]{1,0:T(8,128)(2,1)} %get-tuple-element.102) | non-fusion elementwise | flops 2359296 | bytes 14155776 | tf_op jit(solution)/shard_map/convert_element_type | solution.py:1276
  650.8 4.5 convert_element_type.27
  655.3 3.0 place_half.3
  (66 shorter events, 21.1 us)
Async XLA Ops:
  7.2 6.3 copy-start.4
  7.2 6.4 copy-start.6
  7.2 7.0 %copy-start.7 = (f32[768]{0:T(1024)S(1)}, f32[768]{0:T(1024)}, u32[]{:S(2)}) copy-start(f32[768]{0:T(1024)} %param.18) | copy-start | bytes 9220
  7.2 636.1 %all-reduce.3.cloned.1.call-start = ((), (), s32[]{:S(2)}) async-start(), calls=%async_computation | async-start | bytes 18874368 | tf_op jit(solution)/shard_map/psum | solution.py:1252
  10.5 10.0 %copy-start.5 = (f32[1536]{0:T(1024)S(1)}, f32[1536]{0:T(1024)}, u32[]{:S(2)}) copy-start(f32[1536]{0:T(1024)} %param.20) | copy-start | bytes 18436
  10.5 37.7 %collective-permute-start = (bf16[1024,768]{1,0:T(8,128)(2,1)S(1)}, bf16[1024,768]{1,0:T(8,128)(2,1)S(1)}, u32[]{:S(2)}, u32[]{:S(2)}) collective-permute-start(bf16[1024,768]{1,0:T(8,128)(2,1)S(1)} %get-tuple-element.105), channel_id=1, source_target_pairs={{0,1},{1,0},{2,3},{3,2},{4,5},{5,4},{6,7},{7,6},{8,9},{9,8},{10,11... | collective-permute-start | bytes 4718600 | tf_op jit(solution)/shard_map/ppermute | solution.py:1186
  13.5 34.6 %collective-permute-start.2 = (s32[2,1024]{1,0:T(2,128)S(1)}, s32[2,1024]{1,0:T(2,128)S(1)}, u32[]{:S(2)}, u32[]{:S(2)}) collective-permute-start(s32[2,1024]{1,0:T(2,128)S(1)} %constant_dynamic-slice_fusion), channel_id=1, source_target_pairs={{0,1},{1,0},{2,3},{3,2},{4,5},{5,4},{6,7},{7,6},{8,9},{9,8},{10,11... | collective-permute-start | bytes 24584 | tf_op jit(solution)/shard_map/ppermute | solution.py:1186
  48.2 3.3 copy-start.1
  48.2 35.9 %collective-permute-start.1 = (bf16[1024,768]{1,0:T(8,128)(2,1)}, bf16[1024,768]{1,0:T(8,128)(2,1)S(1)}, u32[]{:S(2)}, u32[]{:S(2)}) collective-permute-start(bf16[1024,768]{1,0:T(8,128)(2,1)} %get-tuple-element.55), channel_id=1, source_target_pairs={{0,1},{1,0},{2,3},{3,2},{4,5},{5,4},{6,7},{7,6},{8,9},{9,8},{10,11... | collective-permute-start | bytes 4718600 | tf_op jit(solution)/shard_map/ppermute | solution.py:1186
  60.0 25.6 %copy-start.8 = (f32[768]{0:T(1024)S(1)}, f32[768]{0:T(1024)}, u32[]{:S(2)}) copy-start(f32[768]{0:T(1024)} %param.22) | copy-start | bytes 9220
  60.0 26.1 %copy-start.9 = (f32[768]{0:T(1024)S(1)}, f32[768]{0:T(1024)}, u32[]{:S(2)}) copy-start(f32[768]{0:T(1024)} %param.23) | copy-start | bytes 9220
  60.0 26.7 %copy-start.10 = (f32[768]{0:T(1024)S(1)}, f32[768]{0:T(1024)}, u32[]{:S(2)}) copy-start(f32[768]{0:T(1024)} %param.24) | copy-start | bytes 9220
  60.0 27.3 %copy-start.11 = (f32[768]{0:T(1024)S(1)}, f32[768]{0:T(1024)}, u32[]{:S(2)}) copy-start(f32[768]{0:T(1024)} %param.28) | copy-start | bytes 9220
  60.0 28.6 %copy-start.2 = (bf16[1024,768]{1,0:T(8,128)(2,1)S(1)}, bf16[1024,768]{1,0:T(8,128)(2,1)}, u32[]{:S(2)}) copy-start(bf16[1024,768]{1,0:T(8,128)(2,1)} %copy-done.1) | copy-start | bytes 4718596
  84.1 30.5 %copy-start = (bf16[1024,768]{1,0:T(8,128)(2,1)}, bf16[1024,768]{1,0:T(8,128)(2,1)S(1)}, u32[]{:S(2)}) copy-start(bf16[1024,768]{1,0:T(8,128)(2,1)S(1)} %collective-permute-done.1.x_ref) | copy-start | bytes 4718596
  84.1 68.7 %collective-permute-start.3 = (bf16[2,1024,768]{2,1,0:T(8,128)(2,1)}, bf16[2,1024,768]{2,1,0:T(8,128)(2,1)}, u32[]{:S(2)}, u32[]{:S(2)}) collective-permute-start(bf16[2,1024,768]{2,1,0:T(8,128)(2,1)} %constant_dynamic-slice_fusion.1), channel_id=1, source_target_pairs={{0,1},{1,0},{2,3},{3,2},{4,5},{5,4},{6,7},{7,6},{8,9},{9,8},{10,11... | collective-permute-start | bytes 9437192 | tf_op jit(solution)/shard_map/ppermute | solution.py:1186
  152.8 185.5 %copy-start.12 = (s32[2,8]{1,0:T(2,128)S(1)}, s32[2,8]{1,0:T(2,128)}, u32[]{:S(2)}) copy-start(s32[2,8]{1,0:T(2,128)} %convert_reduce_fusion) | copy-start | bytes 196
  337.1 95.9 %collective-permute-start.4 = (bf16[2048,768]{1,0:T(8,128)(2,1)}, bf16[2048,768]{1,0:T(8,128)(2,1)}, u32[]{:S(2)}, u32[]{:S(2)}) collective-permute-start(bf16[2048,768]{1,0:T(8,128)(2,1)} %get-tuple-element.71), channel_id=1, source_target_pairs={{0,1},{1,0},{2,3},{3,2},{4,5},{5,4},{6,7},{7,6},{8,9},{9,8},{10,11... | collective-permute-start | bytes 9437192 | tf_op jit(solution)/shard_map/ppermute | solution.py:1186
  483.1 172.2 %collective-permute-start.5 = (bf16[2048,768]{1,0:T(8,128)(2,1)}, bf16[2048,768]{1,0:T(8,128)(2,1)S(1)}, u32[]{:S(2)}, u32[]{:S(2)}) collective-permute-start(bf16[2048,768]{1,0:T(8,128)(2,1)} %get-tuple-element.81), channel_id=1, source_target_pairs={{0,1},{1,0},{2,3},{3,2},{4,5},{5,4},{6,7},{7,6},{8,9},{9,8},{10,11... | collective-permute-start | bytes 9437192 | tf_op jit(solution)/shard_map/ppermute | solution.py:1186
  643.3 7.5 %copy-start.3 = (bf16[3072,768]{1,0:T(8,128)(2,1)S(1)}, bf16[3072,768]{1,0:T(8,128)(2,1)}, u32[]{:S(2)}) copy-start(bf16[3072,768]{1,0:T(8,128)(2,1)} %get-tuple-element.103) | copy-start | bytes 14155780
Sparse Core Ops, SparseCore 0:
  339.0 240.6 all-reduce.2
